TPU v7x, 256 devices: a whole 4x4x8 slice. The times are simulated.
256 devices in a mesh: row: 8 (over y, z_lo), col: 32 (over x, z_hi, core).
Axes of the slice: x: 4, y: 4, z: 8 (z_hi: 4, z_lo: 2; z = z_hi * 2 + z_lo), core: 2. Of those that a mesh axis runs over, the one named last changes fastest.
Arguments:
- atoms: bfloat16 [393216, 128], P(('row', 'col')), may hold values from -48 to 48
- window_offsets: int32 [12288], P(('row', 'col')), may hold values from -64 to -32
- atom_token: int32 [393216], P(('row', 'col')), may hold values from 0 to 32767, as said below
- w_query: bfloat16 [128, 128], replicated, may hold values from -0.5 to 0.5
- w_key: bfloat16 [128, 128], replicated, may hold values from -0.5 to 0.5
- w_value: bfloat16 [128, 128], replicated, may hold values from -0.5 to 0.5
- w_out: bfloat16 [128, 128], replicated, may hold values from -0.5 to 0.5
- w_token: bfloat16 [128, 384], replicated, may hold values from -0.5 to 0.5
- gain_token: bfloat16 [384], replicated, may hold values from 0.099609375 to 1.8984375
- w_pair: bfloat16 [384, 320], replicated, may hold values from -0.3125 to 0.3125
- w_outer: bfloat16 [1024, 128], replicated, may hold values from -0.1875 to 0.1875
Outputs:
- pair_slab: bfloat16 [64, 32768, 128], P('row', 'col')
Inputs may be any that keep to these rules, and one draw needn't show every extreme that they name: `atom_token`: Non-decreasing; token t's first atom lies between t*12 and t*12 + 11, and for t a positive multiple of 128 strictly after t*12; every token has at least one atom.
All inputs are finite; a program needn't handle non-finite values.
Results may differ from a plain program's by a relative error of at most 0.017.
Values may be sent and summed in bfloat16 or wider, within the bound.
A program may use at most 128 MiB of HBM per device.

v0:
```python
import jax
import jax.numpy as jnp
from jax import lax
from jax.sharding import PartitionSpec as P

HEADS = 4
CZ = 128
CO = 32
QB = 32
KW = 128
RIM = 64
TOK_DEV = 128
R_DEV = 8


def extended(value, sides, width):
    for axis, dim in sides:
        count, length = (lax.axis_size(axis), value.shape[dim])
        up = [(i, (i + 1) % count) for i in range(count - 1)]
        down = [(j, i) for i, j in up]
        last = lax.slice_in_dim(value, length - width, length, axis=dim)
        first = lax.slice_in_dim(value, 0, width, axis=dim)
        before = lax.ppermute(last, axis, up)
        after = lax.ppermute(first, axis, down)
        value = jnp.concatenate([before, value, after], axis=dim)
    return value


def passed_along(value, axis, steps):
    count = lax.axis_size(axis)
    first, last = (max(0, -steps), min(count, count - steps))
    return lax.ppermute(value, axis, [(source, source + steps) for source in range(first, last)])


def window_attend(queries, blocks, inside):
    features = queries.shape[-1]
    head_size = features // HEADS
    block_count = queries.shape[0] // QB
    query_heads = queries.reshape(block_count, QB, HEADS, head_size)
    key_heads = blocks[:, :, :features].reshape(block_count, KW, HEADS, head_size)
    value_heads = blocks[:, :, features:].reshape(block_count, KW, HEADS, head_size)
    scores = jnp.einsum(
        "bqhd,bkhd->bhqk", query_heads, key_heads, preferred_element_type=jnp.float32
    ) * head_size ** (-0.5)
    scores = jnp.where(inside[:, None, None, :], scores, -1e30)
    row_max = jnp.max(scores, axis=-1, keepdims=True)
    lifted = jnp.exp(scores - row_max)
    weights = (lifted / jnp.sum(lifted, axis=-1, keepdims=True)).astype(jnp.bfloat16)
    mixed_heads = jnp.einsum(
        "bhqk,bkhd->bqhd", weights, value_heads, preferred_element_type=jnp.float32
    )
    return mixed_heads.astype(jnp.bfloat16).reshape(block_count * QB, features)


def normalize(single, gain_token):
    centre = single - jnp.mean(single, axis=1, keepdims=True)
    variance = jnp.mean(centre * centre, axis=1, keepdims=True)
    return (centre * lax.rsqrt(variance + 1e-05) * gain_token.astype(jnp.float32)).astype(
        jnp.bfloat16
    )


def outer_pairs(left_rows, right_rows, w_outer):
    mixing = jnp.dot(
        left_rows[:, CZ:], w_outer.reshape(CO, CO * CZ), preferred_element_type=jnp.float32
    )
    mixing = mixing.astype(jnp.bfloat16).reshape(-1, CO, CZ)
    pair_grid = jnp.einsum(
        "jn,inc->ijc", right_rows[:, CZ:], mixing, preferred_element_type=jnp.float32
    )
    pair_grid = (
        pair_grid
        + left_rows[:, :CZ].astype(jnp.float32)[:, None, :]
        + right_rows[:, :CZ].astype(jnp.float32)[None]
    )
    return pair_grid.astype(jnp.bfloat16)


def body(
    atoms,
    window_offsets,
    atom_token,
    w_query,
    w_key,
    w_value,
    w_out,
    w_token,
    gain_token,
    w_pair,
    w_outer,
):
    atom_rows = atoms.shape[0]
    device = lax.axis_index(("row", "col"))
    device_count = lax.axis_size(("row", "col"))
    queries = jnp.dot(atoms, w_query, preferred_element_type=jnp.float32).astype(jnp.bfloat16)
    joined = jnp.concatenate([w_key, w_value], axis=1)
    key_values = jnp.dot(atoms, joined, preferred_element_type=jnp.float32).astype(jnp.bfloat16)
    padded = extended(key_values, ((("row", "col"), 0),), RIM)
    block_count = atom_rows // QB
    starts = jnp.arange(block_count, dtype=jnp.int32) * QB + window_offsets + RIM
    window_index = starts[:, None] + jnp.arange(KW, dtype=jnp.int32)[None, :]
    blocks = padded[window_index]
    positions = window_index - RIM + device * atom_rows
    inside = (positions >= 0) & (positions < atom_rows * device_count)
    attended = window_attend(queries, blocks, inside)
    update = (
        atoms.astype(jnp.float32) + jnp.dot(attended, w_out, preferred_element_type=jnp.float32)
    ).astype(jnp.bfloat16)
    hidden = jax.nn.relu(jnp.dot(update, w_token, preferred_element_type=jnp.float32)).astype(
        jnp.bfloat16
    )
    first_token = device * TOK_DEV - 1
    local_slot = atom_token - first_token
    one_hot = (local_slot[None, :] == jnp.arange(TOK_DEV + 1, dtype=jnp.int32)[:, None]).astype(
        jnp.bfloat16
    )
    totals = jnp.dot(one_hot, hidden, preferred_element_type=jnp.float32)
    counts = jnp.sum(one_hot.astype(jnp.float32), axis=1)
    spill_total, spill_count = passed_along((totals[:1], counts[:1]), ("row", "col"), -1)
    own_totals = totals[1:].at[TOK_DEV - 1].add(spill_total[0])
    own_counts = counts[1:].at[TOK_DEV - 1].add(spill_count[0])
    token_norm = normalize(own_totals / own_counts[:, None], gain_token)
    projected = jnp.dot(token_norm, w_pair, preferred_element_type=jnp.float32).astype(jnp.bfloat16)
    row_index = lax.axis_index("row")
    col_index = lax.axis_index("col")
    row_count = lax.axis_size("row")
    column_rows = TOK_DEV * row_count
    everything = lax.all_gather(projected, ("row", "col"), axis=0, tiled=True)
    left_rows = lax.dynamic_slice_in_dim(everything, row_index * R_DEV, R_DEV, 0)[:, : CZ + CO]
    right_rows = lax.dynamic_slice_in_dim(everything, col_index * column_rows, column_rows, 0)[
        :, CZ + CO :
    ]
    return outer_pairs(left_rows, right_rows, w_outer)


def solution(mesh):
    placed = (
        P(("row", "col"), None),
        P(("row", "col")),
        P(("row", "col")),
        P(),
        P(),
        P(),
        P(),
        P(),
        P(),
        P(),
        P(),
    )
    return jax.shard_map(
        body, mesh=mesh, in_specs=placed, out_specs=P("row", "col", None), check_vma=False
    )
```

profile of v0, /device:TPU:65, one launch (start us, length us, event | category | flops | bytes accessed | tf_op | source)
XLA Modules:
  0.0 539.9 jit_solution(11615910442514377667)
XLA Ops:
  6.5 0.7 broadcast_subtract_fusion
  7.5 0.6 slice.82
  8.0 2.6 collective-permute-start.3
  10.6 1.4 fusion.3
  12.1 1.9 collective-permute-start.1
  14.1 6.0 %collective-permute-start = (bf16[64,256]{0,1:T(8,128)(2,1)S(1)}, bf16[64,256]{0,1:T(8,128)(2,1)S(1)}, u32[]{:S(2)}, u32[]{:S(2)}) collective-permute-start(bf16[64,256]{0,1:T(8,128)(2,1)S(1)} %get-tuple-element.32), channel_id=1, source_target_pairs={{0,1},{1,2},{2,3},{3,4},{4,5},{5,6},{6,7},{7,8},{8,9},{9,10},{10,1... | collective-permute-start | bytes 98312 | tf_op jit(solution)/shard_map/ppermute | solution.py:23
  20.1 0.7 add_add_fusion.1
  20.8 1.2 convolution_convert_fusion.2
  22.2 0.7 convert_element_type.65
  22.9 1.8 reshape.164
  24.7 0.9 concatenate.11
  25.6 0.6 copy.37
  26.2 25.0 %gather_fusion = bf16[6144,256]{1,0:T(8,128)(2,1)} fusion(bf16[1664,256]{1,0:T(8,128)(2,1)S(1)} %copy.37, s32[6144]{0:T(1024)S(1)} %fusion.26), kind=kCustom, calls=%fused_computation | custom fusion | bytes 6316032 | tf_op jit(solution)/shard_map/gather | solution.py:102
  51.1 3.4 fusion.36
  54.6 1.9 copy.54
  56.5 1.6 copy.53
  58.1 2.0 fusion.6
  60.0 9.0 %fusion.38 = (f32[48,4,32]{2,1,0:T(4,128)S(1)}, f32[48,4,32,128]{3,2,1,0:T(8,128)S(1)}) fusion(f32[48,4,32,128]{3,2,1,0:T(8,128)S(1)} %fusion.6, pred[48,128]{1,0:T(8,128)(4,1)S(1)} %fusion.29), kind=kOutput, calls=%fused_computation.66 | output fusion | flops 4718719 | bytes 6322176 | tf_op jit(solution)/shard_map/sub | solution.py:47
  69.1 1.3 fusion.12
  70.4 1.0 copy.42
  71.4 1.5 reshape.151
  73.3 0.7 fusion.13
  74.0 1.9 collective-permute-start.2
  75.9 0.6 add_dynamic-update-slice_fusion
  76.6 4.4 collective-permute-done.2
  81.4 0.9 convolution_convert_fusion.4
  82.5 443.2 %all-gather.2.cloned.1.call-done = bf16[32768,320]{1,0:T(8,128)(2,1)} async-done(((bf16[128,320]{1,0:T(8,128)(2,1)}), bf16[32768,320]{1,0:T(8,128)(2,1)}) %all-gather.2.cloned.1.call-update) | async-done | bytes 20971536 | tf_op jit(solution)/shard_map/all_gather | solution.py:128
  525.7 1.2 dynamic-slice_convert_fusion
  527.2 0.7 dynamic-slice_convert_fusion.1
  527.9 0.8 fusion.15
  528.7 1.9 fusion.1
  530.6 2.4 copy.47
  (33 shorter events, 1.6 us)
Async XLA Ops:
  6.5 74.9 %copy-start = (bf16[384,320]{0,1:T(8,128)(2,1)S(1)}, bf16[384,320]{0,1:T(8,128)(2,1)}, u32[]{:S(2)}) copy-start(bf16[384,320]{0,1:T(8,128)(2,1)} %param.24) | copy-start | bytes 737284
  6.5 519.2 %all-gather.2.cloned.1.call-start = ((), (), s32[]{:S(2)}) async-start(), calls=%async_computation | async-start | bytes 25264128 | tf_op jit(solution)/shard_map/all_gather | solution.py:128
  8.0 67.9 %collective-permute-start.3 = (f32[1]{0:T(128)}, f32[1]{0:T(128)}, u32[]{:S(2)}, u32[]{:S(2)}) collective-permute-start(f32[1]{0:T(128)} %slice.82), channel_id=1, source_target_pairs={{1,0},{2,1},{3,2},{4,3},{5,4},{6,5},{7,6},{8,7},{9,8},{10,9},{11,1... | collective-permute-start | bytes 20 | tf_op jit(solution)/shard_map/ppermute | solution.py:32
  12.1 12.6 %collective-permute-start.1 = (bf16[64,256]{0,1:T(8,128)(2,1)S(1)}, bf16[64,256]{0,1:T(8,128)(2,1)S(1)}, u32[]{:S(2)}, u32[]{:S(2)}) collective-permute-start(bf16[64,256]{0,1:T(8,128)(2,1)S(1)} %get-tuple-element.31), channel_id=1, source_target_pairs={{1,0},{2,1},{3,2},{4,3},{5,4},{6,5},{7,6},{8,7},{9,8},{10,9},{11,1... | collective-permute-start | bytes 98312 | tf_op jit(solution)/shard_map/ppermute | solution.py:24
  14.1 10.6 %collective-permute-start = (bf16[64,256]{0,1:T(8,128)(2,1)S(1)}, bf16[64,256]{0,1:T(8,128)(2,1)S(1)}, u32[]{:S(2)}, u32[]{:S(2)}) collective-permute-start(bf16[64,256]{0,1:T(8,128)(2,1)S(1)} %get-tuple-element.32), channel_id=1, source_target_pairs={{0,1},{1,2},{2,3},{3,4},{4,5},{5,6},{6,7},{7,8},{8,9},{9,10},{10,1... | collective-permute-start | bytes 98312 | tf_op jit(solution)/shard_map/ppermute | solution.py:23
  60.0 9.1 %copy-start.2 = (bf16[48,128,128]{1,2,0:T(8,128)(2,1)S(1)}, bf16[48,128,128]{1,2,0:T(8,128)(2,1)}, u32[]{:S(2)}) copy-start(bf16[48,128,128]{1,2,0:T(8,128)(2,1)} %copy.53) | copy-start | bytes 4718596
  70.4 2.6 copy-start.1
  70.4 2.6 copy-start.4
  70.4 2.9 copy-start.5
  71.4 11.0 %copy-start.3 = (bf16[1024,128]{1,0:T(8,128)(2,1)S(1)}, bf16[1024,128]{1,0:T(8,128)(2,1)}, u32[]{:S(2)}) copy-start(bf16[1024,128]{1,0:T(8,128)(2,1)} %param.25) | copy-start | bytes 786436
  74.0 7.0 %collective-permute-start.2 = (f32[1,384]{1,0:T(1,128)S(1)}, f32[1,384]{1,0:T(1,128)S(1)}, u32[]{:S(2)}, u32[]{:S(2)}) collective-permute-start(f32[1,384]{1,0:T(1,128)S(1)} %slice.95), channel_id=1, source_target_pairs={{1,0},{2,1},{3,2},{4,3},{5,4},{6,5},{7,6},{8,7},{9,8},{10,9},{11,1... | collective-permute-start | bytes 4616 | tf_op jit(solution)/shard_map/ppermute | solution.py:32
Sparse Core Ops, SparseCore 0:
  82.5 443.1 all-gather.1
where the time goes:
time: 544 us; the launch traced here: 540 us
  waiting for transfers between devices  448 us (82%)
  local copies, waits for them, and re-layouts  41.2 us (8%)
  other arithmetic  14.4 us (3%)
  between operations  13.7 us (3%)
  starting transfers between devices  12.4 us (2%)
  matrix products  10.5 us (2%)
    all_gather x1, waiting for transfers between devices, body(): everything = lax.all_gather(projected, ('row', 'col'), axis=0, tiled=True)  443 us
    gather x1, local copies, waits for them, and re-layouts, body(): blocks = padded[window_index]  25 us
  transfers between devices with their start and end apart: 5, of which 2 were waited for; matrix products, arithmetic and copies ran while one was open for 10% of the time, Pallas kernels for 0%

commit v1 on v0

v1 whole, which is shorter than its diff:
```python
import jax
import jax.numpy as jnp
from jax import lax
from jax.experimental import pallas as pl
from jax.experimental.pallas import tpu as pltpu
from jax.sharding import PartitionSpec as P

AW = 128
HEADS = 4
TW = 384
CZ = 128
CO = 32
QB = 32
RIM = 64
ROWS = 8
COLS = 32
DEVICES = ROWS * COLS
ATOMS_DEV = 1536
TOK_DEV = 128
EXT = ATOMS_DEV + 2 * RIM
GROUP = 128
GROUPS = ATOMS_DEV // GROUP
KEYS = GROUP + 2 * RIM
HALF = 64
BLK = HALF + HALF // 4
WIDE = TW + 128
EXP_SCALE = float(32 ** -0.5 * 1.4426950408889634)
MESH = pl.DeviceIdType.MESH
NT = (((1,), (1,)), ((), ()))


def dot(a, b):
    return jnp.dot(a, b, preferred_element_type=jnp.float32)


def place(device):
    return (lax.div(device, COLS), lax.rem(device, COLS))


def attend_group(g, edge_low, edge_high, off, keys, queries, values, att):
    k = keys[GROUP * g : GROUP * g + KEYS, :]
    q = queries[:, GROUP * g : GROUP * g + GROUP]
    lane = lax.broadcasted_iota(jnp.int32, (1, GROUP), 1)
    start = jnp.zeros((1, GROUP), jnp.int32)
    for b in range(GROUP // QB):
        start = jnp.where(lane // QB == b, QB * b + RIM + off[GROUP // QB * g + b], start)
    key = lax.broadcasted_iota(jnp.int32, (KEYS, GROUP), 0)
    inside = (key >= start) & (key < start + 128)
    if g == 0:
        inside &= key >= edge_low
    if g == GROUPS - 1:
        inside &= key < edge_high
    bias = jnp.where(inside, 0.0, -1e30)
    zero = jnp.zeros((AW // HEADS, GROUP), jnp.bfloat16)
    outs = []
    for pair in range(2):
        sides = []
        for h in (2 * pair, 2 * pair + 1):
            head = [zero] * HEADS
            head[h] = q[32 * h : 32 * h + 32, :]
            sides.append(jnp.concatenate(head, axis=0))
        scores = dot(k, jnp.concatenate(sides, axis=1))
        scores = scores + jnp.concatenate([bias, bias], axis=1)
        top = jnp.max(scores, axis=0, keepdims=True)
        lifted = jnp.exp2((scores - top) * EXP_SCALE).astype(jnp.bfloat16)
        mixed = dot(values[pair, :, GROUP * g : GROUP * g + KEYS], lifted)
        scaled = mixed[:64] * (1.0 / mixed[64:65])
        outs += [scaled[:32, :GROUP], scaled[32:, GROUP:]]
    att[GROUP * g : GROUP * g + GROUP, :] = jnp.concatenate(outs, axis=0).T.astype(jnp.bfloat16)


def hidden_rows(lo, hi, ext, att, w_out, w_token, hid):
    mixed = dot(att[lo:hi, :], w_out[...])
    update = (ext[RIM + lo : RIM + hi, :].astype(jnp.float32) + mixed).astype(jnp.bfloat16)
    hid[lo:hi, :TW] = jnp.maximum(dot(update, w_token[...]), 0.0).astype(jnp.bfloat16)


def pooled_rows(first, count, lo, hi, device, token, hid):
    slot = token[:, lo:hi] - device * TOK_DEV
    rows = lax.broadcasted_iota(jnp.int32, (count, hi - lo), 0) + first
    one_hot = jnp.where(rows == slot, 1.0, 0.0).astype(jnp.bfloat16)
    return dot(one_hot, hid[lo:hi, :])


def token_normed(pooled, gain):
    count = pooled[:, TW:]
    single = pooled[:, :TW] / jnp.concatenate([count] * 3, axis=1)
    centre = single - jnp.mean(single, axis=1, keepdims=True)
    variance = jnp.mean(centre * centre, axis=1, keepdims=True)
    return (centre * lax.rsqrt(variance + 1e-05) * gain).astype(jnp.bfloat16)


def embed_kernel(
    atoms, off, token, wq, wk, wv, w_out, w_token_hbm, gain, w_pair_hbm,
    gathered, left_rows,
    ext, keys, queries, values, att, hid, w_token, w_pair, w_right,
    spill_out, spill_in, block, left_all, left_in,
    own_sem, load_sem, halo_send, halo_recv, spill_send, spill_recv,
    gather_send, gather_recv, left_send, left_recv, out_sem,
):
    row = lax.axis_index("row")
    col = lax.axis_index("col")
    me = row * COLS + col
    before = lax.rem(me + DEVICES - 1, DEVICES)
    after = lax.rem(me + 1, DEVICES)
    group_col = lax.div(me, ROWS)
    slot = lax.rem(me, ROWS)
    keeps = jnp.where(group_col == col, 1, 0)

    def signal(device):
        pl.semaphore_signal(barrier, inc=1, device_id=place(device), device_id_type=MESH)

    barrier = pltpu.get_barrier_semaphore()
    signal(before)
    signal(after)
    for k in range(ROWS):
        @pl.when(ROWS * col + k != me)
        def _():
            signal(ROWS * col + k)

    @pl.when(col != 0)
    def _():
        signal(row * COLS)

    @pl.when((col == 0) & (row != 0))
    def _():
        signal(0)

    own = pltpu.make_async_copy(atoms, ext.at[pl.ds(RIM, ATOMS_DEV)], own_sem)
    own.start()
    loads = [
        pltpu.make_async_copy(w_token_hbm, w_token, load_sem.at[0]),
        pltpu.make_async_copy(w_pair_hbm, w_pair, load_sem.at[1]),
    ]
    for load in loads:
        load.start()

    both = jnp.concatenate([wq[...], wv[...]], axis=1).astype(jnp.float32).T.astype(jnp.bfloat16)
    hid[:, TW:] = jnp.ones((ATOMS_DEV, WIDE - TW), jnp.bfloat16)
    for pair in range(2):
        values[pair, 64:, :] = jnp.ones((16, EXT), jnp.bfloat16)
    own.wait()
    for lo in range(0, ATOMS_DEV, 512):
        x = ext[RIM + lo : RIM + lo + 512, :]
        keys[RIM + lo : RIM + lo + 512, :] = dot(x, wk[...]).astype(jnp.bfloat16)
    for lo in range(128, ATOMS_DEV, 256):
        hi = min(lo + 256, ATOMS_DEV)
        x = ext[lo:hi, :]
        vt = lax.dot_general(both[AW:], x, NT, preferred_element_type=jnp.float32).astype(jnp.bfloat16)
        values[0, :64, lo:hi] = vt[:64]
        values[1, :64, lo:hi] = vt[64:]
    for lo in range(0, ATOMS_DEV, 512):
        x = ext[RIM + lo : RIM + lo + 512, :]
        queries[:, lo : lo + 512] = lax.dot_general(
            both[:AW], x, NT, preferred_element_type=jnp.float32
        ).astype(jnp.bfloat16)

    is_leader = jnp.where(col == 0, 1, 0)
    is_first = jnp.where(me == 0, 1, 0)
    pl.semaphore_wait(barrier, 2 + ROWS - keeps + (COLS - 1) * is_leader + (ROWS - 1) * is_first)

    halo = [
        pltpu.make_async_remote_copy(
            src_ref=atoms.at[pl.ds(ATOMS_DEV - RIM, RIM)], dst_ref=ext.at[pl.ds(0, RIM)],
            send_sem=halo_send.at[0], recv_sem=halo_recv.at[0],
            device_id=place(after), device_id_type=MESH,
        ),
        pltpu.make_async_remote_copy(
            src_ref=atoms.at[pl.ds(0, RIM)], dst_ref=ext.at[pl.ds(EXT - RIM, RIM)],
            send_sem=halo_send.at[1], recv_sem=halo_recv.at[1],
            device_id=place(before), device_id_type=MESH,
        ),
    ]
    for copy in halo:
        copy.start()

    edge_low = jnp.where(me == 0, RIM, 0)
    edge_high = jnp.where(me == DEVICES - 1, KEYS - RIM, KEYS)

    def attend(g):
        attend_group(g, edge_low, edge_high, off, keys, queries, values, att)

    for load in loads:
        load.wait()
    w_right[:, :CZ] = w_pair[:, CZ + CO : 2 * CZ + CO]
    w_right[:, CZ:] = jnp.concatenate([w_pair[:, 2 * CZ + CO :]] * 4, axis=1)

    for g in range(1, 6):
        attend(g)

    for copy in halo:
        copy.wait()
    for lo in (0, EXT - RIM):
        keys[lo : lo + RIM, :] = dot(ext[lo : lo + RIM, :], wk[...]).astype(jnp.bfloat16)
    for lo in (0, EXT - 128):
        vt = lax.dot_general(
            both[AW:], ext[lo : lo + 128, :], NT, preferred_element_type=jnp.float32
        ).astype(jnp.bfloat16)
        values[0, :64, lo : lo + 128] = vt[:64]
        values[1, :64, lo : lo + 128] = vt[64:]
    attend(0)
    attend(6)

    lane = lax.broadcasted_iota(jnp.int32, (16, CZ), 1)
    sends = []

    def finish(half, pooled):
        normed = token_normed(pooled, gain[...].astype(jnp.float32))
        right = dot(normed, w_right[...])
        packed = right[:16, CZ:]
        for m in range(1, 4):
            packed = jnp.where(lane // CO == m, right[16 * m : 16 * m + 16, CZ:], packed)
        block[half, :HALF, :] = right[:, :CZ].astype(jnp.bfloat16)
        block[half, HALF:, :] = packed.astype(jnp.bfloat16)
        for i in range(ROWS):
            to_row = lax.rem(slot + i, ROWS)
            copy = pltpu.make_async_remote_copy(
                src_ref=block.at[half], dst_ref=gathered.at[slot, half],
                send_sem=gather_send.at[half, i], recv_sem=gather_recv.at[half, slot],
                device_id=(to_row, group_col), device_id_type=MESH,
            )
            mine = (to_row == row) & (group_col == col)

            @pl.when(jnp.logical_not(mine))
            def _():
                copy.start()

            @pl.when(mine)
            def _():
                pltpu.make_async_copy(
                    block.at[half], gathered.at[slot, half], gather_send.at[half, i]
                ).start()

            sends.append((copy, mine, half, i))
        return normed

    hidden_rows(0, 896, ext, att, w_out, w_token, hid)
    pooled = pooled_rows(-16, 80, 0, 896, me, token, hid)
    spill_out[...] = pooled[8:16]
    spill = pltpu.make_async_remote_copy(
        src_ref=spill_out, dst_ref=spill_in, send_sem=spill_send, recv_sem=spill_recv,
        device_id=place(before), device_id_type=MESH,
    )
    spill.start()
    normed = finish(0, pooled[16:])

    def left_copy(source, to, index):
        return pltpu.make_async_remote_copy(
            src_ref=source, dst_ref=left_in, send_sem=left_send.at[index], recv_sem=left_recv,
            device_id=to, device_id_type=MESH,
        )

    @pl.when(me == 0)
    def _():
        left = dot(normed, w_pair[:, : 2 * CZ])
        for r in range(ROWS):
            rows = left[8 * r : 8 * r + 8]
            left_all[r] = jnp.concatenate([rows[:, :CZ], rows[:, CZ:]], axis=0).astype(jnp.bfloat16)
        left_in[...] = left_all[0]
        for r in range(1, ROWS):
            left_copy(left_all.at[r], (r, 0), r).start()

    for g in range(7, 12):
        attend(g)
    hidden_rows(896, ATOMS_DEV, ext, att, w_out, w_token, hid)
    pooled = pooled_rows(HALF, HALF, 768, ATOMS_DEV, me, token, hid)
    spill.wait()
    pooled = jnp.concatenate([pooled[:56], pooled[56:] + spill_in[...]], axis=0)
    finish(1, pooled)

    @pl.when(me == 0)
    def _():
        for r in range(1, ROWS):
            left_copy(left_all.at[r], (r, 0), r).wait_send()

    @pl.when(me != 0)
    def _():
        left_copy(left_in, (row, 0), 0).wait_recv()

    @pl.when(col == 0)
    def _():
        for c in range(1, COLS):
            left_copy(left_in, (row, c), c).start()
        for c in range(1, COLS):
            left_copy(left_in, (row, c), c).wait_send()

    result = pltpu.make_async_copy(left_in, left_rows, out_sem)
    result.start()
    for half in range(2):
        for k in range(ROWS):
            source = ROWS * col + k

            @pl.when(source != me)
            def _():
                pltpu.make_async_remote_copy(
                    src_ref=block.at[half], dst_ref=gathered.at[k, half],
                    send_sem=gather_send.at[half, 0], recv_sem=gather_recv.at[half, k],
                    device_id=place(source), device_id_type=MESH,
                ).wait_recv()

    for copy, mine, half, i in sends:
        @pl.when(jnp.logical_not(mine))
        def _():
            copy.wait_send()

        @pl.when(mine)
        def _():
            pltpu.make_async_copy(
                block.at[half], gathered.at[slot, half], gather_send.at[half, i]
            ).wait()
    result.wait()


def pair_kernel(gathered, left_rows, w_outer, out, base, result, sems):
    left = left_rows[:8, :]
    outer = left_rows[8:, :CO]
    spread = lax.broadcasted_iota(jnp.int32, (CO, CO * CO), 1) // CO
    spread = jnp.where(spread == lax.broadcasted_iota(jnp.int32, (CO, CO * CO), 0), 1.0, 0.0)
    wide = dot(outer, spread.astype(jnp.bfloat16))
    n = lax.broadcasted_iota(jnp.int32, (CO, CO * CO), 0)
    mine = lax.rem(lax.broadcasted_iota(jnp.int32, (CO, CO * CO), 1), CO) == n
    expanded = [jnp.where(mine, wide[i : i + 1], 0.0).astype(jnp.bfloat16) for i in range(8)]
    mixing = dot(jnp.concatenate(expanded, axis=0), w_outer[...]).astype(jnp.bfloat16)
    eye = jnp.where(
        lax.broadcasted_iota(jnp.int32, (CZ, CZ), 0) == lax.broadcasted_iota(jnp.int32, (CZ, CZ), 1), 1.0, 0.0
    ).astype(jnp.bfloat16)
    for i in range(8):
        base[:CZ, CZ * i : CZ * i + CZ] = eye
        for k in range(4):
            base[CZ + CO * k : CZ + CO * k + CO, CZ * i : CZ * i + CZ] = mixing[CO * i : CO * i + CO]
    left = left.astype(jnp.float32)
    lane = lax.broadcasted_iota(jnp.int32, (16, CZ), 1)
    copies = []
    for k in range(ROWS):
        parts = []
        for half in range(2):
            packed = gathered[k, half, HALF:, :].astype(jnp.float32)
            outer_rows = [jnp.where(lane // CO == m, packed, 0.0) for m in range(4)]
            outer_rows = jnp.concatenate(outer_rows, axis=0).astype(jnp.bfloat16)
            parts.append(jnp.concatenate([gathered[k, half, :HALF, :], outer_rows], axis=1))
        rows = jnp.concatenate(parts, axis=0)
        for i in range(0, 8, 2):
            grid = dot(rows, base[:, CZ * i : CZ * i + 2 * CZ])
            for j in range(2):
                total = grid[:, CZ * j : CZ * j + CZ] + left[i + j : i + j + 1]
                result[i + j, TOK_DEV * k : TOK_DEV * k + TOK_DEV, :] = total.astype(jnp.bfloat16)
        copy = pltpu.make_async_copy(
            result.at[:, pl.ds(TOK_DEV * k, TOK_DEV)], out.at[:, pl.ds(TOK_DEV * k, TOK_DEV)], sems.at[k]
        )
        copy.start()
        copies.append(copy)
    for copy in copies:
        copy.wait()


def body(
    atoms, window_offsets, atom_token, w_query, w_key, w_value, w_out, w_token, gain_token, w_pair, w_outer
):
    vmem = pl.BlockSpec(memory_space=pltpu.VMEM)
    smem = pl.BlockSpec(memory_space=pltpu.SMEM)
    anywhere = pl.BlockSpec(memory_space=pl.ANY)
    dma = pltpu.SemaphoreType.DMA
    bf16, f32 = jnp.bfloat16, jnp.float32
    gathered, left_rows = pl.pallas_call(
        embed_kernel,
        out_shape=[
            jax.ShapeDtypeStruct((ROWS, 2, BLK, CZ), bf16),
            jax.ShapeDtypeStruct((16, CZ), bf16),
        ],
        in_specs=[anywhere, smem, vmem, vmem, vmem, vmem, vmem, anywhere, vmem, anywhere],
        out_specs=[anywhere, anywhere],
        scratch_shapes=[
            pltpu.VMEM((EXT, AW), bf16),
            pltpu.VMEM((EXT, AW), bf16),
            pltpu.VMEM((AW, ATOMS_DEV), bf16),
            pltpu.VMEM((2, 80, EXT), bf16),
            pltpu.VMEM((ATOMS_DEV, AW), bf16),
            pltpu.VMEM((ATOMS_DEV, WIDE), bf16),
            pltpu.VMEM((AW, TW), bf16),
            pltpu.VMEM((TW, 2 * CZ + 2 * CO), bf16),
            pltpu.VMEM((TW, 2 * CZ), bf16),
            pltpu.VMEM((8, WIDE), f32),
            pltpu.VMEM((8, WIDE), f32),
            pltpu.VMEM((2, BLK, CZ), bf16),
            pltpu.VMEM((ROWS, 16, CZ), bf16),
            pltpu.VMEM((16, CZ), bf16),
            dma, dma((2,)), dma((2,)), dma((2,)), dma, dma,
            dma((2, ROWS)), dma((2, ROWS)), dma((COLS,)), dma, dma,
        ],
        compiler_params=pltpu.CompilerParams(
            collective_id=0, has_side_effects=True, vmem_limit_bytes=32 * 1024 * 1024
        ),
        name="embed",
    )(
        atoms, window_offsets, atom_token.reshape(1, -1), w_query, w_key, w_value, w_out, w_token,
        gain_token.reshape(1, -1), w_pair,
    )
    return pl.pallas_call(
        pair_kernel,
        out_shape=jax.ShapeDtypeStruct((8, ROWS * TOK_DEV, CZ), bf16),
        in_specs=[vmem, vmem, vmem],
        out_specs=anywhere,
        scratch_shapes=[
            pltpu.VMEM((2 * CZ, 8 * CZ), bf16),
            pltpu.VMEM((8, ROWS * TOK_DEV, CZ), bf16),
            dma((ROWS,)),
        ],
        compiler_params=pltpu.CompilerParams(vmem_limit_bytes=32 * 1024 * 1024),
        name="pair",
    )(gathered, left_rows, w_outer)


def solution(mesh):
    split = P(("row", "col"))
    placed = (P(("row", "col"), None), split, split) + (P(),) * 8
    return jax.shard_map(
        body, mesh=mesh, in_specs=placed, out_specs=P("row", "col", None), check_vma=False
    )
```

time: 544 us -> 55.3 us (0.10)
  waiting for transfers between devices: 448 us -> 0 us
  Pallas kernels: 0 us -> 45.2 us
  local copies, waits for them, and re-layouts: 41.2 us -> 9.05 us
  other arithmetic: 14.4 us -> 0 us
  between operations: 13.7 us -> 0.04 us
  starting transfers between devices: 12.4 us -> 0 us
  matrix products: 10.5 us -> 0 us
    all_gather x1 -> x0, waiting for transfers between devices: 443 us -> none  [body(): everything = lax.all_gather(projected, ('row', 'col'), axis=0, tiled=True)]
    pallas_call x0 -> x2, Pallas kernels: none -> 45.2 us  [the longest x1 43.2 us: body(): pl.pallas_call(embed_kernel, out_shape=[jax.ShapeDtypeStruct((ROWS, 2, BL...]
    gather x1 -> x0, local copies, waits for them, and re-layouts: 25 us -> none  [body(): blocks = padded[window_index]]
    ppermute x4 -> x0, starting transfers between devices: 12.4 us -> none  [the longest x1 6.01 us: extended(): before = lax.ppermute(last, axis, up)]
    dot_general x9 -> x0, matrix products: 10.5 us -> none  [the longest x1 1.96 us: window_attend(): jnp.einsum('bqhd,bkhd->bhqk', query_heads, key_heads, preferred_element_t...]
    sub x2 -> x0, other arithmetic: 9.78 us -> none  [the longest x1 9.04 us: window_attend(): lifted = jnp.exp(scores - row_max)]
  transfers between devices with their start and end apart: 5 -> 0, of which waited for: 2 -> 0; matrix products, arithmetic and copies ran while one was open for 10% -> 0% of each run, Pallas kernels for 0% -> 0%
where the time goes in v1:
time: 55.3 us; the launch traced here: 54.3 us
  Pallas kernels  45.2 us (82%)
  local copies, waits for them, and re-layouts  9.05 us (16%)
    pallas_call x1, Pallas kernels, body(): pl.pallas_call(embed_kernel, out_shape=[jax.ShapeDtypeStruct((ROWS, 2, BL...  43.2 us
    unnamed x17, local copies, waits for them, and re-layouts  7.66 us
    pallas_call x1, Pallas kernels, body(): pl.pallas_call(pair_kernel, out_shape=jax.ShapeDtypeStruct((8, ROWS * TOK...  2 us

profile of v1, /device:TPU:65, one launch (start us, length us, event | category | flops | bytes accessed | tf_op | source)
XLA Modules:
  0.0 54.3 jit_solution(14508613006366435370)
XLA Ops:
  0.0 0.7 %reshape.7.gain = bf16[1,384]{1,0:T(2,128)(2,1)S(1)} reshape(bf16[384]{0:T(512)(128)(2,1)} %param.19) | data formatting | bytes 1536 | tf_op jit(solution)/shard_map/reshape | solution.py:396
  0.7 0.7 %reshape.6.token = s32[1,1536]{1,0:T(1,128)S(1)} reshape(s32[1536]{0:T(1024)} %param.13) | data formatting | bytes 12288 | tf_op jit(solution)/shard_map/reshape | solution.py:395
  1.4 1.1 %copy.12.w_pair_hbm = bf16[384,320]{1,0:T(8,128)(2,1)S(1)} copy(bf16[384,320]{0,1:T(8,128)(2,1)} %param.20) | data formatting | bytes 491520 | tf_op args[9]
  2.5 0.0 copy-start
  2.6 1.0 %copy-done = bf16[1536,128]{1,0:T(8,128)(2,1)S(1)} copy-done((bf16[1536,128]{1,0:T(8,128)(2,1)S(1)}, bf16[1536,128]{1,0:T(8,128)(2,1)}, u32[]{:S(2)}) %copy-start) | copy-done | bytes 393240
  3.5 0.0 copy-start.2
  3.5 0.9 %copy-done.2 = bf16[128,384]{1,0:T(8,128)(2,1)S(1)} copy-done((bf16[128,384]{1,0:T(8,128)(2,1)S(1)}, bf16[128,384]{1,0:T(8,128)(2,1)}, u32[]{:S(2)}) %copy-start.2) | copy-done | bytes 98328
  4.4 0.0 copy-start.3
  4.4 0.8 %copy-done.3 = bf16[128,128]{1,0:T(8,128)(2,1)S(1)} copy-done((bf16[128,128]{1,0:T(8,128)(2,1)S(1)}, bf16[128,128]{1,0:T(8,128)(2,1)}, u32[]{:S(2)}) %copy-start.3) | copy-done | bytes 32792
  5.2 0.0 copy-start.4
  5.2 0.8 %copy-done.4 = bf16[128,128]{1,0:T(8,128)(2,1)S(1)} copy-done((bf16[128,128]{1,0:T(8,128)(2,1)S(1)}, bf16[128,128]{1,0:T(8,128)(2,1)}, u32[]{:S(2)}) %copy-start.4) | copy-done | bytes 32792
  5.9 0.0 copy-start.5
  6.0 0.8 %copy-done.5 = bf16[128,128]{1,0:T(8,128)(2,1)S(1)} copy-done((bf16[128,128]{1,0:T(8,128)(2,1)S(1)}, bf16[128,128]{1,0:T(8,128)(2,1)}, u32[]{:S(2)}) %copy-start.5) | copy-done | bytes 32792
  6.7 0.0 copy-start.6
  6.7 0.8 %copy-done.6 = bf16[128,128]{1,0:T(8,128)(2,1)S(1)} copy-done((bf16[128,128]{1,0:T(8,128)(2,1)S(1)}, bf16[128,128]{1,0:T(8,128)(2,1)}, u32[]{:S(2)}) %copy-start.6) | copy-done | bytes 32792
  7.5 0.0 copy-start.7
  7.5 0.7 %copy-done.7 = s32[48]{0:T(128)S(1)} copy-done((s32[48]{0:T(128)S(1)}, s32[48]{0:T(128)}, u32[]{:S(2)}) %copy-start.7) | copy-done | bytes 216
  8.1 43.2 %embed.1 = (bf16[8,2,80,128]{3,2,1,0:T(8,128)(2,1)S(1)}, bf16[16,128]{1,0:T(8,128)(2,1)S(1)}) custom-call(bf16[1536,128]{1,0:T(8,128)(2,1)S(1)} %copy-done, s32[48]{0:T(128)S(1)} %copy-done.7, s32[1,1536]{1,0:T(1,128)S(1)} %reshape.6.token, bf16[128,128]{1,0:T(8,128)(2,1)S(1)} %copy-done.3, bf16[128,128]{1,0:T(8,128)(2,1)S(1)} %copy-done.4, ...), custom_call_target="tpu_custom_call" | custom-call | tf_op jit(solution)/shard_map/embed/pallas_call | solution.py:364
  51.4 0.0 copy-start.1
  51.4 0.9 %copy-done.1 = bf16[1024,128]{1,0:T(8,128)(2,1)S(1)} copy-done((bf16[1024,128]{1,0:T(8,128)(2,1)S(1)}, bf16[1024,128]{1,0:T(8,128)(2,1)}, u32[]{:S(2)}) %copy-start.1) | copy-done | bytes 262168
  52.3 2.0 %pair.1 = bf16[8,1024,128]{2,1,0:T(8,128)(2,1)} custom-call(bf16[8,2,80,128]{3,2,1,0:T(8,128)(2,1)S(1)} %get-tuple-element.7.gathered, bf16[16,128]{1,0:T(8,128)(2,1)S(1)} %get-tuple-element.8.left_rows, bf16[1024,128]{1,0:T(8,128)(2,1)S(1)} %copy-done.1), custom_call_target="tpu_custom_call" | custom-call | tf_op jit(solution)/shard_map/pair/pallas_call | solution.py:398
Async XLA Ops:
  2.5 1.0 %copy-start = (bf16[1536,128]{1,0:T(8,128)(2,1)S(1)}, bf16[1536,128]{1,0:T(8,128)(2,1)}, u32[]{:S(2)}) copy-start(bf16[1536,128]{1,0:T(8,128)(2,1)} %atoms.1) | copy-start | bytes 1179652
  3.5 0.9 %copy-start.2 = (bf16[128,384]{1,0:T(8,128)(2,1)S(1)}, bf16[128,384]{1,0:T(8,128)(2,1)}, u32[]{:S(2)}) copy-start(bf16[128,384]{1,0:T(8,128)(2,1)} %w_token_hbm.1) | copy-start | bytes 294916
  4.4 0.8 %copy-start.3 = (bf16[128,128]{1,0:T(8,128)(2,1)S(1)}, bf16[128,128]{1,0:T(8,128)(2,1)}, u32[]{:S(2)}) copy-start(bf16[128,128]{1,0:T(8,128)(2,1)} %wq.1) | copy-start | bytes 98308
  5.2 0.8 %copy-start.4 = (bf16[128,128]{1,0:T(8,128)(2,1)S(1)}, bf16[128,128]{1,0:T(8,128)(2,1)}, u32[]{:S(2)}) copy-start(bf16[128,128]{1,0:T(8,128)(2,1)} %wk.1) | copy-start | bytes 98308
  5.9 0.8 %copy-start.5 = (bf16[128,128]{1,0:T(8,128)(2,1)S(1)}, bf16[128,128]{1,0:T(8,128)(2,1)}, u32[]{:S(2)}) copy-start(bf16[128,128]{1,0:T(8,128)(2,1)} %wv.1) | copy-start | bytes 98308
  6.7 0.8 %copy-start.6 = (bf16[128,128]{1,0:T(8,128)(2,1)S(1)}, bf16[128,128]{1,0:T(8,128)(2,1)}, u32[]{:S(2)}) copy-start(bf16[128,128]{1,0:T(8,128)(2,1)} %w_out.1) | copy-start | bytes 98308
  7.5 0.7 %copy-start.7 = (s32[48]{0:T(128)S(1)}, s32[48]{0:T(128)}, u32[]{:S(2)}) copy-start(s32[48]{0:T(128)} %off.1) | copy-start | bytes 580
  51.4 1.0 %copy-start.1 = (bf16[1024,128]{1,0:T(8,128)(2,1)S(1)}, bf16[1024,128]{1,0:T(8,128)(2,1)}, u32[]{:S(2)}) copy-start(bf16[1024,128]{1,0:T(8,128)(2,1)} %w_outer.1) | copy-start | bytes 786436

commit v2 on v1

--- a/solution.py
+++ b/solution.py
@@ -76,7 +76,7 @@
 
 
 def pooled_rows(first, count, lo, hi, device, token, hid):
-    slot = token[:, lo:hi] - device * TOK_DEV
+    slot = token[...].reshape(1, ATOMS_DEV)[:, lo:hi] - device * TOK_DEV
     rows = lax.broadcasted_iota(jnp.int32, (count, hi - lo), 0) + first
     one_hot = jnp.where(rows == slot, 1.0, 0.0).astype(jnp.bfloat16)
     return dot(one_hot, hid[lo:hi, :])
@@ -91,12 +91,13 @@
 
 
 def embed_kernel(
-    atoms, off, token, wq, wk, wv, w_out, w_token_hbm, gain, w_pair_hbm,
+    atoms, off_hbm, token_hbm, wq_hbm, wk_hbm, wv_hbm, w_out_hbm, w_token_hbm, gain_hbm, w_pair_hbm,
     gathered, left_rows,
-    ext, keys, queries, values, att, hid, w_token, w_pair, w_right,
+    off, token, wq, wk, wv, w_out, w_token, gain, w_pair,
+    ext, keys, queries, values, att, hid, w_right,
     spill_out, spill_in, block, left_all, left_in,
     own_sem, load_sem, halo_send, halo_recv, spill_send, spill_recv,
-    gather_send, gather_recv, left_send, left_recv, out_sem,
+    first_send, first_recv, local_sem, pass_send, pass_recv, left_send, left_recv, out_sem,
 ):
     row = lax.axis_index("row")
     col = lax.axis_index("col")
@@ -105,7 +106,10 @@
     after = lax.rem(me + 1, DEVICES)
     group_col = lax.div(me, ROWS)
     slot = lax.rem(me, ROWS)
-    keeps = jnp.where(group_col == col, 1, 0)
+    my_y, my_z = lax.div(row, 2), lax.rem(row, 2)
+    relay_y = lax.rem(lax.div(col, 8) + lax.div(slot, 2), 4)
+    held = 2 * lax.rem(my_y + 4 - lax.rem(col, 4), 4)
+    keeps = jnp.where((group_col == col) & (relay_y == my_y), 1, 0)
 
     def signal(device):
         pl.semaphore_signal(barrier, inc=1, device_id=place(device), device_id_type=MESH)
@@ -113,12 +117,18 @@
     barrier = pltpu.get_barrier_semaphore()
     signal(before)
     signal(after)
-    for k in range(ROWS):
-        @pl.when(ROWS * col + k != me)
+    for k in range(2):
+        @pl.when(ROWS * col + held + k != me)
         def _():
-            signal(ROWS * col + k)
-
-    @pl.when(col != 0)
+            signal(ROWS * col + held + k)
+    for i in range(1, 4):
+        signal((2 * lax.rem(my_y + i, 4) + my_z) * COLS + col)
+
+    @pl.when(lax.rem(col, 8) != 0)
+    def _():
+        signal(me - lax.rem(col, 8))
+
+    @pl.when((lax.rem(col, 8) == 0) & (col != 0))
     def _():
         signal(row * COLS)
 
@@ -128,12 +138,15 @@
 
     own = pltpu.make_async_copy(atoms, ext.at[pl.ds(RIM, ATOMS_DEV)], own_sem)
     own.start()
-    loads = [
-        pltpu.make_async_copy(w_token_hbm, w_token, load_sem.at[0]),
-        pltpu.make_async_copy(w_pair_hbm, w_pair, load_sem.at[1]),
+    pieces = [
+        (wq_hbm, wq), (wk_hbm, wk), (wv_hbm, wv), (off_hbm, off), (w_out_hbm, w_out),
+        (token_hbm, token), (w_token_hbm, w_token), (gain_hbm, gain), (w_pair_hbm, w_pair),
     ]
+    loads = [pltpu.make_async_copy(a, b, load_sem.at[i]) for i, (a, b) in enumerate(pieces)]
     for load in loads:
         load.start()
+    for load in loads[:3]:
+        load.wait()
 
     both = jnp.concatenate([wq[...], wv[...]], axis=1).astype(jnp.float32).T.astype(jnp.bfloat16)
     hid[:, TW:] = jnp.ones((ATOMS_DEV, WIDE - TW), jnp.bfloat16)
@@ -155,9 +168,10 @@
             both[:AW], x, NT, preferred_element_type=jnp.float32
         ).astype(jnp.bfloat16)
 
+    is_head = jnp.where(lax.rem(col, 8) == 0, 1, 0)
     is_leader = jnp.where(col == 0, 1, 0)
     is_first = jnp.where(me == 0, 1, 0)
-    pl.semaphore_wait(barrier, 2 + ROWS - keeps + (COLS - 1) * is_leader + (ROWS - 1) * is_first)
+    pl.semaphore_wait(barrier, 2 + 2 - keeps + 3 + 7 * is_head + 3 * is_leader + 7 * is_first)
 
     halo = [
         pltpu.make_async_remote_copy(
@@ -180,10 +194,11 @@
     def attend(g):
         attend_group(g, edge_low, edge_high, off, keys, queries, values, att)
 
-    for load in loads:
+    for load in loads[3:]:
         load.wait()
-    w_right[:, :CZ] = w_pair[:, CZ + CO : 2 * CZ + CO]
-    w_right[:, CZ:] = jnp.concatenate([w_pair[:, 2 * CZ + CO :]] * 4, axis=1)
+    w_right[:CZ, :] = w_pair[CZ + CO : 2 * CZ + CO, :]
+    for m in range(4):
+        w_right[CZ + CO * m : CZ + CO * m + CO, :] = w_pair[2 * CZ + CO :, :]
 
     for g in range(1, 6):
         attend(g)
@@ -202,24 +217,52 @@
     attend(6)
 
     lane = lax.broadcasted_iota(jnp.int32, (16, CZ), 1)
-    sends = []
+
+    def first_copy(half, i):
+        return pltpu.make_async_remote_copy(
+            src_ref=block.at[half], dst_ref=gathered.at[half, slot],
+            send_sem=first_send.at[half, i], recv_sem=first_recv.at[half, lax.rem(slot, 2)],
+            device_id=(2 * relay_y + i, group_col), device_id_type=MESH,
+        )
+
+    def local_copy(half):
+        return pltpu.make_async_copy(block.at[half], gathered.at[half, slot], local_sem.at[half])
+
+    def pass_copy(half, i, start):
+        return pltpu.make_async_remote_copy(
+            src_ref=gathered.at[half, pl.ds(start, 2)], dst_ref=gathered.at[half, pl.ds(start, 2)],
+            send_sem=pass_send.at[half, i], recv_sem=pass_recv.at[half, i],
+            device_id=(2 * lax.rem(my_y + i, 4) + my_z, col), device_id_type=MESH,
+        )
+
+    def pass_on(half):
+        for k in range(2):
+            @pl.when(ROWS * col + held + k != me)
+            def _():
+                pltpu.make_async_remote_copy(
+                    src_ref=block.at[half], dst_ref=gathered.at[half, held + k],
+                    send_sem=first_send.at[half, 0], recv_sem=first_recv.at[half, k],
+                    device_id=place(ROWS * col + held + k), device_id_type=MESH,
+                ).wait_recv()
+
+        @pl.when(keeps == 1)
+        def _():
+            local_copy(half).wait()
+
+        for i in range(1, 4):
+            pass_copy(half, i, held).start()
 
     def finish(half, pooled):
-        normed = token_normed(pooled, gain[...].astype(jnp.float32))
-        right = dot(normed, w_right[...])
+        normed = token_normed(pooled, gain[...].reshape(1, TW).astype(jnp.float32))
+        right = lax.dot_general(normed, w_right[...], NT, preferred_element_type=jnp.float32)
         packed = right[:16, CZ:]
         for m in range(1, 4):
             packed = jnp.where(lane // CO == m, right[16 * m : 16 * m + 16, CZ:], packed)
         block[half, :HALF, :] = right[:, :CZ].astype(jnp.bfloat16)
         block[half, HALF:, :] = packed.astype(jnp.bfloat16)
-        for i in range(ROWS):
-            to_row = lax.rem(slot + i, ROWS)
-            copy = pltpu.make_async_remote_copy(
-                src_ref=block.at[half], dst_ref=gathered.at[slot, half],
-                send_sem=gather_send.at[half, i], recv_sem=gather_recv.at[half, slot],
-                device_id=(to_row, group_col), device_id_type=MESH,
-            )
-            mine = (to_row == row) & (group_col == col)
+        for i in range(2):
+            copy = first_copy(half, i)
+            mine = (keeps == 1) & (my_z == i)
 
             @pl.when(jnp.logical_not(mine))
             def _():
@@ -227,11 +270,8 @@
 
             @pl.when(mine)
             def _():
-                pltpu.make_async_copy(
-                    block.at[half], gathered.at[slot, half], gather_send.at[half, i]
-                ).start()
-
-            sends.append((copy, mine, half, i))
+                local_copy(half).start()
+
         return normed
 
     hidden_rows(0, 896, ext, att, w_out, w_token, hid)
@@ -252,7 +292,7 @@
 
     @pl.when(me == 0)
     def _():
-        left = dot(normed, w_pair[:, : 2 * CZ])
+        left = lax.dot_general(normed, w_pair[: 2 * CZ, :], NT, preferred_element_type=jnp.float32)
         for r in range(ROWS):
             rows = left[8 * r : 8 * r + 8]
             left_all[r] = jnp.concatenate([rows[:, :CZ], rows[:, CZ:]], axis=0).astype(jnp.bfloat16)
@@ -279,35 +319,39 @@
 
     @pl.when(col == 0)
     def _():
-        for c in range(1, COLS):
-            left_copy(left_in, (row, c), c).start()
-        for c in range(1, COLS):
-            left_copy(left_in, (row, c), c).wait_send()
+        for x in range(1, 4):
+            left_copy(left_in, (row, 8 * x), 8 + x).start()
+
+    @pl.when(lax.rem(col, 8) == 0)
+    def _():
+        for c in range(1, 8):
+            left_copy(left_in, (row, col + c), 16 + c).start()
 
     result = pltpu.make_async_copy(left_in, left_rows, out_sem)
     result.start()
     for half in range(2):
-        for k in range(ROWS):
-            source = ROWS * col + k
-
-            @pl.when(source != me)
+        pass_on(half)
+
+    for half in range(2):
+        for i in range(1, 4):
+            theirs = 2 * lax.rem(my_y + 4 - i + 4 - lax.rem(col, 4), 4)
+            pass_copy(half, i, theirs).wait_recv()
+            pass_copy(half, i, held).wait_send()
+        for i in range(2):
+            @pl.when(jnp.logical_not((keeps == 1) & (my_z == i)))
             def _():
-                pltpu.make_async_remote_copy(
-                    src_ref=block.at[half], dst_ref=gathered.at[k, half],
-                    send_sem=gather_send.at[half, 0], recv_sem=gather_recv.at[half, k],
-                    device_id=place(source), device_id_type=MESH,
-                ).wait_recv()
-
-    for copy, mine, half, i in sends:
-        @pl.when(jnp.logical_not(mine))
-        def _():
-            copy.wait_send()
-
-        @pl.when(mine)
-        def _():
-            pltpu.make_async_copy(
-                block.at[half], gathered.at[slot, half], gather_send.at[half, i]
-            ).wait()
+                first_copy(half, i).wait_send()
+
+    @pl.when(col == 0)
+    def _():
+        for x in range(1, 4):
+            left_copy(left_in, (row, 8 * x), 8 + x).wait_send()
+
+    @pl.when(lax.rem(col, 8) == 0)
+    def _():
+        for c in range(1, 8):
+            left_copy(left_in, (row, col + c), 16 + c).wait_send()
+
     result.wait()
 
 
@@ -334,10 +378,10 @@
     for k in range(ROWS):
         parts = []
         for half in range(2):
-            packed = gathered[k, half, HALF:, :].astype(jnp.float32)
+            packed = gathered[half, k, HALF:, :].astype(jnp.float32)
             outer_rows = [jnp.where(lane // CO == m, packed, 0.0) for m in range(4)]
             outer_rows = jnp.concatenate(outer_rows, axis=0).astype(jnp.bfloat16)
-            parts.append(jnp.concatenate([gathered[k, half, :HALF, :], outer_rows], axis=1))
+            parts.append(jnp.concatenate([gathered[half, k, :HALF, :], outer_rows], axis=1))
         rows = jnp.concatenate(parts, axis=0)
         for i in range(0, 8, 2):
             grid = dot(rows, base[:, CZ * i : CZ * i + 2 * CZ])
@@ -357,43 +401,49 @@
     atoms, window_offsets, atom_token, w_query, w_key, w_value, w_out, w_token, gain_token, w_pair, w_outer
 ):
     vmem = pl.BlockSpec(memory_space=pltpu.VMEM)
-    smem = pl.BlockSpec(memory_space=pltpu.SMEM)
+    hbm = pl.BlockSpec(memory_space=pltpu.HBM)
     anywhere = pl.BlockSpec(memory_space=pl.ANY)
     dma = pltpu.SemaphoreType.DMA
     bf16, f32 = jnp.bfloat16, jnp.float32
     gathered, left_rows = pl.pallas_call(
         embed_kernel,
         out_shape=[
-            jax.ShapeDtypeStruct((ROWS, 2, BLK, CZ), bf16),
+            jax.ShapeDtypeStruct((2, ROWS, BLK, CZ), bf16),
             jax.ShapeDtypeStruct((16, CZ), bf16),
         ],
-        in_specs=[anywhere, smem, vmem, vmem, vmem, vmem, vmem, anywhere, vmem, anywhere],
+        in_specs=[hbm] * 10,
         out_specs=[anywhere, anywhere],
         scratch_shapes=[
+            pltpu.SMEM((ATOMS_DEV // QB,), jnp.int32),
+            pltpu.VMEM((ATOMS_DEV,), jnp.int32),
+            pltpu.VMEM((AW, AW), bf16),
+            pltpu.VMEM((AW, AW), bf16),
+            pltpu.VMEM((AW, AW), bf16),
+            pltpu.VMEM((AW, AW), bf16),
+            pltpu.VMEM((AW, TW), bf16),
+            pltpu.VMEM((TW,), bf16),
+            pltpu.VMEM((2 * CZ + 2 * CO, TW), bf16),
             pltpu.VMEM((EXT, AW), bf16),
             pltpu.VMEM((EXT, AW), bf16),
             pltpu.VMEM((AW, ATOMS_DEV), bf16),
             pltpu.VMEM((2, 80, EXT), bf16),
             pltpu.VMEM((ATOMS_DEV, AW), bf16),
             pltpu.VMEM((ATOMS_DEV, WIDE), bf16),
-            pltpu.VMEM((AW, TW), bf16),
-            pltpu.VMEM((TW, 2 * CZ + 2 * CO), bf16),
-            pltpu.VMEM((TW, 2 * CZ), bf16),
+            pltpu.VMEM((2 * CZ, TW), bf16),
             pltpu.VMEM((8, WIDE), f32),
             pltpu.VMEM((8, WIDE), f32),
             pltpu.VMEM((2, BLK, CZ), bf16),
             pltpu.VMEM((ROWS, 16, CZ), bf16),
             pltpu.VMEM((16, CZ), bf16),
-            dma, dma((2,)), dma((2,)), dma((2,)), dma, dma,
-            dma((2, ROWS)), dma((2, ROWS)), dma((COLS,)), dma, dma,
+            dma, dma((9,)), dma((2,)), dma((2,)), dma, dma,
+            dma((2, 2)), dma((2, 2)), dma((2,)), dma((2, 4)), dma((2, 4)), dma((COLS,)), dma, dma,
         ],
         compiler_params=pltpu.CompilerParams(
-            collective_id=0, has_side_effects=True, vmem_limit_bytes=32 * 1024 * 1024
+            collective_id=0, has_side_effects=True, vmem_limit_bytes=60 * 1024 * 1024
         ),
         name="embed",
     )(
-        atoms, window_offsets, atom_token.reshape(1, -1), w_query, w_key, w_value, w_out, w_token,
-        gain_token.reshape(1, -1), w_pair,
+        atoms, window_offsets, atom_token, w_query, w_key, w_value, w_out, w_token, gain_token, w_pair.T,
     )
     return pl.pallas_call(
         pair_kernel,
@@ -405,7 +455,7 @@
             pltpu.VMEM((8, ROWS * TOK_DEV, CZ), bf16),
             dma((ROWS,)),
         ],
-        compiler_params=pltpu.CompilerParams(vmem_limit_bytes=32 * 1024 * 1024),
+        compiler_params=pltpu.CompilerParams(vmem_limit_bytes=60 * 1024 * 1024),
         name="pair",
     )(gathered, left_rows, w_outer)
 

time: 55.3 us -> 33.2 us (0.60); the launches traced: 54.3 us -> 32.8 us
  Pallas kernels: 45.2 us -> 32.8 us
  local copies, waits for them, and re-layouts: 9.05 us -> 0 us
    pallas_call x1, Pallas kernels: 43.2 us -> 29.8 us  [body(): pl.pallas_call(embed_kernel, out_shape=[jax.ShapeDtypeStruct((2, ROWS, BL...]
    unnamed x17 -> x0, local copies, waits for them, and re-layouts: 7.66 us -> none
    reshape x2 -> x0, local copies, waits for them, and re-layouts: 1.38 us -> none  [the longest x1 0.7 us: body(): atom_token.reshape(1, -1)]
    pallas_call x1, Pallas kernels: 2 us -> 3.06 us  [body(): pl.pallas_call(pair_kernel, out_shape=jax.ShapeDtypeStruct((8, ROWS * TOK...]
where the time goes in v2:
time: 33.2 us; the launch traced here: 32.8 us
  Pallas kernels  32.8 us (99%)
    pallas_call x1, Pallas kernels, body(): pl.pallas_call(embed_kernel, out_shape=[jax.ShapeDtypeStruct((2, ROWS, BL...  29.8 us
    pallas_call x1, Pallas kernels, body(): pl.pallas_call(pair_kernel, out_shape=jax.ShapeDtypeStruct((8, ROWS * TOK...  3.06 us

profile of v2, /device:TPU:65, one launch (start us, length us, event | category | flops | bytes accessed | tf_op | source)
XLA Modules:
  0.0 32.8 jit_solution(15180694980581536881)
XLA Ops:
  0.0 29.8 %embed.1 = (bf16[2,8,80,128]{3,2,1,0:T(8,128)(2,1)}, bf16[16,128]{1,0:T(8,128)(2,1)}) custom-call(bf16[1536,128]{1,0:T(8,128)(2,1)} %atoms.1, s32[48]{0:T(128)} %off_hbm.1, s32[1536]{0:T(1024)} %token_hbm.1, bf16[128,128]{1,0:T(8,128)(2,1)} %wq_hbm.1, bf16[128,128]{1,0:T(8,128)(2,1)} %wk_hbm.1, bf16[128,128]{1,0:T(8,128)(2,1)} %wv_hbm.1, ...), custom_call_target="tpu_custom_call" | custom-call | tf_op jit(solution)/shard_map/embed/pallas_call | solution.py:408
  29.8 3.1 %pair.1 = bf16[8,1024,128]{2,1,0:T(8,128)(2,1)} custom-call(bf16[2,8,80,128]{3,2,1,0:T(8,128)(2,1)} %get-tuple-element.7.gathered, bf16[16,128]{1,0:T(8,128)(2,1)} %get-tuple-element.8.left_rows, bf16[1024,128]{1,0:T(8,128)(2,1)} %w_outer.1), custom_call_target="tpu_custom_call" | custom-call | tf_op jit(solution)/shard_map/pair/pallas_call | solution.py:448

commit v3 on v2

--- a/solution.py
+++ b/solution.py
@@ -91,13 +91,14 @@
 
 
 def embed_kernel(
-    atoms, off_hbm, token_hbm, wq_hbm, wk_hbm, wv_hbm, w_out_hbm, w_token_hbm, gain_hbm, w_pair_hbm,
-    gathered, left_rows,
-    off, token, wq, wk, wv, w_out, w_token, gain, w_pair,
+    atoms, off_hbm, token_hbm, wq_hbm, wk_hbm, wv_hbm, w_out_hbm, w_token_hbm, gain_hbm, w_pair_hbm, w_outer_hbm,
+    result,
+    off, token, wq, wk, wv, w_out, w_token, gain, w_pair, w_outer,
+    gathered, base,
     ext, keys, queries, values, att, hid, w_right,
     spill_out, spill_in, block, left_all, left_in,
     own_sem, load_sem, halo_send, halo_recv, spill_send, spill_recv,
-    first_send, first_recv, local_sem, pass_send, pass_recv, left_send, left_recv, out_sem,
+    first_send, first_recv, local_sem, pass_send, pass_recv, left_send, left_recv,
 ):
     row = lax.axis_index("row")
     col = lax.axis_index("col")
@@ -141,6 +142,7 @@
     pieces = [
         (wq_hbm, wq), (wk_hbm, wk), (wv_hbm, wv), (off_hbm, off), (w_out_hbm, w_out),
         (token_hbm, token), (w_token_hbm, w_token), (gain_hbm, gain), (w_pair_hbm, w_pair),
+        (w_outer_hbm, w_outer),
     ]
     loads = [pltpu.make_async_copy(a, b, load_sem.at[i]) for i, (a, b) in enumerate(pieces)]
     for load in loads:
@@ -196,6 +198,9 @@
 
     for load in loads[3:]:
         load.wait()
+    eye = lax.broadcasted_iota(jnp.int32, (CZ, CZ), 0) == lax.broadcasted_iota(jnp.int32, (CZ, CZ), 1)
+    for i in range(8):
+        base[:CZ, CZ * i : CZ * i + CZ] = jnp.where(eye, 1.0, 0.0).astype(jnp.bfloat16)
     w_right[:CZ, :] = w_pair[CZ + CO : 2 * CZ + CO, :]
     for m in range(4):
         w_right[CZ + CO * m : CZ + CO * m + CO, :] = w_pair[2 * CZ + CO :, :]
@@ -300,20 +305,17 @@
         for r in range(1, ROWS):
             left_copy(left_all.at[r], (r, 0), r).start()
 
-    for g in range(7, 12):
+    for g in range(7, 11):
         attend(g)
+
+    attend(11)
     hidden_rows(896, ATOMS_DEV, ext, att, w_out, w_token, hid)
     pooled = pooled_rows(HALF, HALF, 768, ATOMS_DEV, me, token, hid)
     spill.wait()
     pooled = jnp.concatenate([pooled[:56], pooled[56:] + spill_in[...]], axis=0)
     finish(1, pooled)
 
-    @pl.when(me == 0)
-    def _():
-        for r in range(1, ROWS):
-            left_copy(left_all.at[r], (r, 0), r).wait_send()
-
-    @pl.when(me != 0)
+    @pl.when((col == 0) & (me != 0))
     def _():
         left_copy(left_in, (row, 0), 0).wait_recv()
 
@@ -321,43 +323,69 @@
     def _():
         for x in range(1, 4):
             left_copy(left_in, (row, 8 * x), 8 + x).start()
-
-    @pl.when(lax.rem(col, 8) == 0)
+        for c in range(1, 8):
+            left_copy(left_in, (row, c), 16 + c).start()
+
+    pass_on(0)
+
+    @pl.when((lax.rem(col, 8) == 0) & (col != 0))
+    def _():
+        left_copy(left_in, (row, 0), 0).wait_recv()
+
+    @pl.when((lax.rem(col, 8) == 0) & (col != 0))
     def _():
         for c in range(1, 8):
             left_copy(left_in, (row, col + c), 16 + c).start()
 
-    result = pltpu.make_async_copy(left_in, left_rows, out_sem)
-    result.start()
-    for half in range(2):
-        pass_on(half)
-
-    for half in range(2):
+    pass_on(1)
+
+    @pl.when(lax.rem(col, 8) != 0)
+    def _():
+        left_copy(left_in, (row, 0), 0).wait_recv()
+
+    mix_left(left_in, w_outer, base)
+    left = left_in[:8, :].astype(jnp.float32)
+
+    def pair_rows(half, start):
+        pair_block(gathered, half, start, base, left, result)
+
+    def arrived(half):
         for i in range(1, 4):
             theirs = 2 * lax.rem(my_y + 4 - i + 4 - lax.rem(col, 4), 4)
             pass_copy(half, i, theirs).wait_recv()
+            pair_rows(half, theirs)
+
+    pair_rows(0, held)
+    arrived(0)
+    pair_rows(1, held)
+    arrived(1)
+
+    @pl.when(me == 0)
+    def _():
+        for r in range(1, ROWS):
+            left_copy(left_all.at[r], (r, 0), r).wait_send()
+
+    @pl.when(col == 0)
+    def _():
+        for x in range(1, 4):
+            left_copy(left_in, (row, 8 * x), 8 + x).wait_send()
+
+    @pl.when(lax.rem(col, 8) == 0)
+    def _():
+        for c in range(1, 8):
+            left_copy(left_in, (row, col + c), 16 + c).wait_send()
+
+    for half in range(2):
+        for i in range(1, 4):
             pass_copy(half, i, held).wait_send()
         for i in range(2):
             @pl.when(jnp.logical_not((keeps == 1) & (my_z == i)))
             def _():
                 first_copy(half, i).wait_send()
 
-    @pl.when(col == 0)
-    def _():
-        for x in range(1, 4):
-            left_copy(left_in, (row, 8 * x), 8 + x).wait_send()
-
-    @pl.when(lax.rem(col, 8) == 0)
-    def _():
-        for c in range(1, 8):
-            left_copy(left_in, (row, col + c), 16 + c).wait_send()
-
-    result.wait()
-
-
-def pair_kernel(gathered, left_rows, w_outer, out, base, result, sems):
-    left = left_rows[:8, :]
-    outer = left_rows[8:, :CO]
+
+def mix_left(left_in, w_outer, base):
+    outer = left_in[8:, :CO]
     spread = lax.broadcasted_iota(jnp.int32, (CO, CO * CO), 1) // CO
     spread = jnp.where(spread == lax.broadcasted_iota(jnp.int32, (CO, CO * CO), 0), 1.0, 0.0)
     wide = dot(outer, spread.astype(jnp.bfloat16))
@@ -365,54 +393,40 @@
     mine = lax.rem(lax.broadcasted_iota(jnp.int32, (CO, CO * CO), 1), CO) == n
     expanded = [jnp.where(mine, wide[i : i + 1], 0.0).astype(jnp.bfloat16) for i in range(8)]
     mixing = dot(jnp.concatenate(expanded, axis=0), w_outer[...]).astype(jnp.bfloat16)
-    eye = jnp.where(
-        lax.broadcasted_iota(jnp.int32, (CZ, CZ), 0) == lax.broadcasted_iota(jnp.int32, (CZ, CZ), 1), 1.0, 0.0
-    ).astype(jnp.bfloat16)
     for i in range(8):
-        base[:CZ, CZ * i : CZ * i + CZ] = eye
         for k in range(4):
             base[CZ + CO * k : CZ + CO * k + CO, CZ * i : CZ * i + CZ] = mixing[CO * i : CO * i + CO]
-    left = left.astype(jnp.float32)
+
+
+def pair_block(gathered, half, start, base, left, result):
     lane = lax.broadcasted_iota(jnp.int32, (16, CZ), 1)
-    copies = []
-    for k in range(ROWS):
-        parts = []
-        for half in range(2):
-            packed = gathered[half, k, HALF:, :].astype(jnp.float32)
-            outer_rows = [jnp.where(lane // CO == m, packed, 0.0) for m in range(4)]
-            outer_rows = jnp.concatenate(outer_rows, axis=0).astype(jnp.bfloat16)
-            parts.append(jnp.concatenate([gathered[half, k, :HALF, :], outer_rows], axis=1))
-        rows = jnp.concatenate(parts, axis=0)
-        for i in range(0, 8, 2):
-            grid = dot(rows, base[:, CZ * i : CZ * i + 2 * CZ])
-            for j in range(2):
-                total = grid[:, CZ * j : CZ * j + CZ] + left[i + j : i + j + 1]
-                result[i + j, TOK_DEV * k : TOK_DEV * k + TOK_DEV, :] = total.astype(jnp.bfloat16)
-        copy = pltpu.make_async_copy(
-            result.at[:, pl.ds(TOK_DEV * k, TOK_DEV)], out.at[:, pl.ds(TOK_DEV * k, TOK_DEV)], sems.at[k]
-        )
-        copy.start()
-        copies.append(copy)
-    for copy in copies:
-        copy.wait()
+    parts = []
+    for k in range(2):
+        packed = gathered[half, start + k, HALF:, :].astype(jnp.float32)
+        outer = [jnp.where(lane // CO == m, packed, 0.0) for m in range(4)]
+        outer = jnp.concatenate(outer, axis=0).astype(jnp.bfloat16)
+        parts.append(jnp.concatenate([gathered[half, start + k, :HALF, :], outer], axis=1))
+    rows = jnp.concatenate(parts, axis=0)
+    for i in range(0, 8, 2):
+        grid = dot(rows, base[:, CZ * i : CZ * i + 2 * CZ])
+        for j in range(2):
+            total = (grid[:, CZ * j : CZ * j + CZ] + left[i + j : i + j + 1]).astype(jnp.bfloat16)
+            for k in range(2):
+                first = pl.multiple_of(TOK_DEV * (start + k) + HALF * half, HALF)
+                result[i + j, pl.ds(first, HALF), :] = total[HALF * k : HALF * k + HALF]
 
 
 def body(
     atoms, window_offsets, atom_token, w_query, w_key, w_value, w_out, w_token, gain_token, w_pair, w_outer
 ):
-    vmem = pl.BlockSpec(memory_space=pltpu.VMEM)
     hbm = pl.BlockSpec(memory_space=pltpu.HBM)
-    anywhere = pl.BlockSpec(memory_space=pl.ANY)
     dma = pltpu.SemaphoreType.DMA
     bf16, f32 = jnp.bfloat16, jnp.float32
-    gathered, left_rows = pl.pallas_call(
+    return pl.pallas_call(
         embed_kernel,
-        out_shape=[
-            jax.ShapeDtypeStruct((2, ROWS, BLK, CZ), bf16),
-            jax.ShapeDtypeStruct((16, CZ), bf16),
-        ],
-        in_specs=[hbm] * 10,
-        out_specs=[anywhere, anywhere],
+        out_shape=pltpu.VMEM((8, ROWS * TOK_DEV, CZ), bf16),
+        in_specs=[hbm] * 11,
+        out_specs=pl.BlockSpec(memory_space=pltpu.VMEM),
         scratch_shapes=[
             pltpu.SMEM((ATOMS_DEV // QB,), jnp.int32),
             pltpu.VMEM((ATOMS_DEV,), jnp.int32),
@@ -423,6 +437,9 @@
             pltpu.VMEM((AW, TW), bf16),
             pltpu.VMEM((TW,), bf16),
             pltpu.VMEM((2 * CZ + 2 * CO, TW), bf16),
+            pltpu.VMEM((CO * CO, CZ), bf16),
+            pltpu.VMEM((2, ROWS, BLK, CZ), bf16),
+            pltpu.VMEM((2 * CZ, 8 * CZ), bf16),
             pltpu.VMEM((EXT, AW), bf16),
             pltpu.VMEM((EXT, AW), bf16),
             pltpu.VMEM((AW, ATOMS_DEV), bf16),
@@ -435,8 +452,8 @@
             pltpu.VMEM((2, BLK, CZ), bf16),
             pltpu.VMEM((ROWS, 16, CZ), bf16),
             pltpu.VMEM((16, CZ), bf16),
-            dma, dma((9,)), dma((2,)), dma((2,)), dma, dma,
-            dma((2, 2)), dma((2, 2)), dma((2,)), dma((2, 4)), dma((2, 4)), dma((COLS,)), dma, dma,
+            dma, dma((10,)), dma((2,)), dma((2,)), dma, dma,
+            dma((2, 2)), dma((2, 2)), dma((2,)), dma((2, 4)), dma((2, 4)), dma((COLS,)), dma,
         ],
         compiler_params=pltpu.CompilerParams(
             collective_id=0, has_side_effects=True, vmem_limit_bytes=60 * 1024 * 1024
@@ -444,20 +461,8 @@
         name="embed",
     )(
         atoms, window_offsets, atom_token, w_query, w_key, w_value, w_out, w_token, gain_token, w_pair.T,
+        w_outer,
     )
-    return pl.pallas_call(
-        pair_kernel,
-        out_shape=jax.ShapeDtypeStruct((8, ROWS * TOK_DEV, CZ), bf16),
-        in_specs=[vmem, vmem, vmem],
-        out_specs=anywhere,
-        scratch_shapes=[
-            pltpu.VMEM((2 * CZ, 8 * CZ), bf16),
-            pltpu.VMEM((8, ROWS * TOK_DEV, CZ), bf16),
-            dma((ROWS,)),
-        ],
-        compiler_params=pltpu.CompilerParams(vmem_limit_bytes=60 * 1024 * 1024),
-        name="pair",
-    )(gathered, left_rows, w_outer)
 
 
 def solution(mesh):

time: 33.2 us -> 31.3 us (0.943)
  Pallas kernels: 32.8 us -> 29.9 us
  local copies, waits for them, and re-layouts: 0 us -> 1.32 us
    pallas_call x2 -> x1, Pallas kernels: 32.8 us -> 29.9 us  [body(): pl.pallas_call(embed_kernel, out_shape=pltpu.VMEM((8, ROWS * TOK_DEV, CZ)...]
    unnamed x0 -> x1, local copies, waits for them, and re-layouts: none -> 1.32 us
where the time goes in v3:
time: 31.3 us; the launch traced here: 31.2 us
  Pallas kernels  29.9 us (96%)
  local copies, waits for them, and re-layouts  1.32 us (4%)
    pallas_call x1, Pallas kernels, body(): pl.pallas_call(embed_kernel, out_shape=pltpu.VMEM((8, ROWS * TOK_DEV, CZ)...  29.9 us
    unnamed x1, local copies, waits for them, and re-layouts  1.32 us

profile of v3, /device:TPU:65, one launch (start us, length us, event | category | flops | bytes accessed | tf_op | source)
XLA Modules:
  0.0 31.2 jit_solution(7201250268488655939)
XLA Ops:
  0.0 29.9 %embed.1 = bf16[8,1024,128]{2,1,0:T(8,128)(2,1)S(1)} custom-call(bf16[1536,128]{1,0:T(8,128)(2,1)} %atoms.1, s32[48]{0:T(128)} %off_hbm.1, s32[1536]{0:T(1024)} %token_hbm.1, bf16[128,128]{1,0:T(8,128)(2,1)} %wq_hbm.1, bf16[128,128]{1,0:T(8,128)(2,1)} %wk_hbm.1, bf16[128,128]{1,0:T(8,128)(2,1)} %wv_hbm.1, bf16[128,128]{1,0:T(8,128)(2,1)} %w_out_hbm.1, ...), custom_call_target="tpu_custom_call" | custom-call | tf_op jit(solution)/shard_map/embed/pallas_call | solution.py:425
  29.9 1.3 %copy.13 = bf16[8,1024,128]{2,1,0:T(8,128)(2,1)} copy(bf16[8,1024,128]{2,1,0:T(8,128)(2,1)S(1)} %embed.1) | data formatting | bytes 4194304

commit v4 on v3

--- a/solution.py
+++ b/solution.py
@@ -20,7 +20,9 @@
 EXT = ATOMS_DEV + 2 * RIM
 GROUP = 128
 GROUPS = ATOMS_DEV // GROUP
-KEYS = GROUP + 2 * RIM
+UNITS = 2 * GROUPS
+AHEAD = 3
+BEHIND = 2
 HALF = 64
 BLK = HALF + HALF // 4
 WIDE = TW + 128
@@ -37,49 +39,92 @@
     return (lax.div(device, COLS), lax.rem(device, COLS))
 
 
-def attend_group(g, edge_low, edge_high, off, keys, queries, values, att):
-    k = keys[GROUP * g : GROUP * g + KEYS, :]
+def dot_nt(a, b):
+    return lax.dot_general(a, b, NT, preferred_element_type=jnp.float32)
+
+
+def turned(w):
+    return w[...].astype(jnp.float32).T.astype(jnp.bfloat16)
+
+
+def unit_scores(unit, keys, queries):
+    g, j = unit // 2, unit % 2
     q = queries[:, GROUP * g : GROUP * g + GROUP]
+    side = (lax.broadcasted_iota(jnp.int32, (HALF, GROUP), 0) // 32 == j) == (
+        lax.broadcasted_iota(jnp.int32, (HALF, GROUP), 1) < HALF
+    )
+    none = jnp.zeros((HALF, GROUP), jnp.bfloat16)
+    heads = [jnp.where(side, q[HALF * t : HALF * t + HALF], none) for t in range(2)]
+    operand = jnp.concatenate(
+        [jnp.concatenate([heads[0], none], axis=1), jnp.concatenate([none, heads[1]], axis=1)], axis=0
+    )
+    return dot(keys[HALF * unit : HALF * unit + 192, :], operand)
+
+
+def unit_softmax(unit, scores, me, off):
     lane = lax.broadcasted_iota(jnp.int32, (1, GROUP), 1)
-    start = jnp.zeros((1, GROUP), jnp.int32)
-    for b in range(GROUP // QB):
-        start = jnp.where(lane // QB == b, QB * b + RIM + off[GROUP // QB * g + b], start)
-    key = lax.broadcasted_iota(jnp.int32, (KEYS, GROUP), 0)
-    inside = (key >= start) & (key < start + 128)
-    if g == 0:
-        inside &= key >= edge_low
-    if g == GROUPS - 1:
-        inside &= key < edge_high
-    bias = jnp.where(inside, 0.0, -1e30)
-    zero = jnp.zeros((AW // HEADS, GROUP), jnp.bfloat16)
-    outs = []
-    for pair in range(2):
-        sides = []
-        for h in (2 * pair, 2 * pair + 1):
-            head = [zero] * HEADS
-            head[h] = q[32 * h : 32 * h + 32, :]
-            sides.append(jnp.concatenate(head, axis=0))
-        scores = dot(k, jnp.concatenate(sides, axis=1))
-        scores = scores + jnp.concatenate([bias, bias], axis=1)
-        top = jnp.max(scores, axis=0, keepdims=True)
-        lifted = jnp.exp2((scores - top) * EXP_SCALE).astype(jnp.bfloat16)
-        mixed = dot(values[pair, :, GROUP * g : GROUP * g + KEYS], lifted)
-        scaled = mixed[:64] * (1.0 / mixed[64:65])
-        outs += [scaled[:32, :GROUP], scaled[32:, GROUP:]]
-    att[GROUP * g : GROUP * g + GROUP, :] = jnp.concatenate(outs, axis=0).T.astype(jnp.bfloat16)
-
-
-def hidden_rows(lo, hi, ext, att, w_out, w_token, hid):
-    mixed = dot(att[lo:hi, :], w_out[...])
-    update = (ext[RIM + lo : RIM + hi, :].astype(jnp.float32) + mixed).astype(jnp.bfloat16)
-    hid[lo:hi, :TW] = jnp.maximum(dot(update, w_token[...]), 0.0).astype(jnp.bfloat16)
+    second = lax.rem(lane // QB, 2) == 1
+    start = jnp.where(second, off[2 * unit + 1] + RIM + QB, off[2 * unit] + RIM)
+    low, high = start, start + 128
+    if unit == 0:
+        low = jnp.maximum(low, jnp.where(me == 0, RIM, 0))
+    if unit == UNITS - 1:
+        high = jnp.minimum(high, jnp.where(me == DEVICES - 1, 128, 192))
+    row = lax.broadcasted_iota(jnp.int32, (HALF, GROUP), 0)
+    enters, stays = row >= low, row + 128 < high
+    parts = []
+    for t in range(2):
+        tile = scores[:, GROUP * t : GROUP * t + GROUP]
+        tile = jnp.concatenate(
+            [jnp.where(enters, tile[:64], -1e30), tile[64:128], jnp.where(stays, tile[128:], -1e30)], axis=0
+        )
+        top = jnp.max(tile, axis=0, keepdims=True)
+        parts.append(jnp.exp2((tile - top) * EXP_SCALE).astype(jnp.bfloat16))
+    return jnp.concatenate(
+        [jnp.concatenate(parts, axis=1), jnp.zeros((HALF, 2 * GROUP), jnp.bfloat16)], axis=0
+    )
+
+
+def group_store(g, mixed, att):
+    left = lax.broadcasted_iota(jnp.int32, (1, GROUP), 1) < HALF
+    for h in range(HEADS):
+        lanes = slice(GROUP * (h // 2), GROUP * (h // 2) + GROUP)
+        a, b = mixed if h % 2 == 0 else mixed[::-1]
+        total = jnp.where(left, a[AW : AW + 1, lanes], b[AW : AW + 1, lanes])
+        value = jnp.where(left, a[32 * h : 32 * h + 32, lanes], b[32 * h : 32 * h + 32, lanes]) * (1.0 / total)
+        if h % 2 == 1:
+            value = pltpu.roll(value, HALF, 1)
+        att[32 * h : 32 * h + 32, GROUP * g : GROUP * g + GROUP] = value.astype(jnp.bfloat16)
+
+
+def attend(groups, me, off, keys, queries, values, att):
+    units = [2 * g + j for g in groups for j in range(2)]
+    scores, lifted, mixed = {}, {}, {}
+    for i in range(len(units) + AHEAD + BEHIND):
+        if i < len(units):
+            scores[i] = unit_scores(units[i], keys, queries)
+        k = i - AHEAD
+        if 0 <= k < len(units):
+            lifted[k] = unit_softmax(units[k], scores.pop(k), me, off)
+        k = i - AHEAD - BEHIND
+        if 0 <= k < len(units):
+            g, j = units[k] // 2, units[k] % 2
+            mixed[j] = dot(values[j, :, GROUP * g : GROUP * g + 2 * GROUP], lifted.pop(k))
+            if j == 1:
+                group_store(g, [mixed[0], mixed[1]], att)
+
+
+def hidden_rows(lo, hi, turned_atoms, att, w_out_t, w_token_t, hid):
+    mixed = dot(w_out_t[...], att[:, lo:hi])
+    update = (turned_atoms[:, lo:hi].astype(jnp.float32) + mixed).astype(jnp.bfloat16)
+    hid[:TW, lo:hi] = jnp.maximum(dot(w_token_t[...], update), 0.0).astype(jnp.bfloat16)
 
 
 def pooled_rows(first, count, lo, hi, device, token, hid):
     slot = token[...].reshape(1, ATOMS_DEV)[:, lo:hi] - device * TOK_DEV
     rows = lax.broadcasted_iota(jnp.int32, (count, hi - lo), 0) + first
     one_hot = jnp.where(rows == slot, 1.0, 0.0).astype(jnp.bfloat16)
-    return dot(one_hot, hid[lo:hi, :])
+    return dot_nt(one_hot, hid[:, lo:hi])
 
 
 def token_normed(pooled, gain):
@@ -95,7 +140,7 @@
     result,
     off, token, wq, wk, wv, w_out, w_token, gain, w_pair, w_outer,
     gathered, base,
-    ext, keys, queries, values, att, hid, w_right,
+    ext, keys, queries, values, att, hid, turned_atoms, w_out_t, w_token_t, w_right,
     spill_out, spill_in, block, left_all, left_in,
     own_sem, load_sem, halo_send, halo_recv, spill_send, spill_recv,
     first_send, first_recv, local_sem, pass_send, pass_recv, left_send, left_recv,
@@ -150,25 +195,34 @@
     for load in loads[:3]:
         load.wait()
 
-    both = jnp.concatenate([wq[...], wv[...]], axis=1).astype(jnp.float32).T.astype(jnp.bfloat16)
-    hid[:, TW:] = jnp.ones((ATOMS_DEV, WIDE - TW), jnp.bfloat16)
-    for pair in range(2):
-        values[pair, 64:, :] = jnp.ones((16, EXT), jnp.bfloat16)
+    one = lax.broadcasted_iota(jnp.int32, (CZ, CZ), 0) == lax.broadcasted_iota(jnp.int32, (CZ, CZ), 1)
+    eye = jnp.where(one, 1.0, 0.0).astype(jnp.bfloat16)
+    value_t = turned(wv)
+    left_side = jnp.concatenate([turned(wq), value_t, eye], axis=0)
+    hid[TW:, :] = jnp.ones((WIDE - TW, ATOMS_DEV), jnp.bfloat16)
+    for j in range(2):
+        values[j, AW:, :] = jnp.ones((16, EXT), jnp.bfloat16)
     own.wait()
     for lo in range(0, ATOMS_DEV, 512):
         x = ext[RIM + lo : RIM + lo + 512, :]
         keys[RIM + lo : RIM + lo + 512, :] = dot(x, wk[...]).astype(jnp.bfloat16)
+    for lo in range(0, ATOMS_DEV, 256):
+        product = dot_nt(left_side, ext[RIM + lo : RIM + lo + 256, :])
+        for h in range(HEADS):
+            rows = slice(32 * h, 32 * h + 32)
+            for part in range(0, 256, GROUP):
+                q = product[rows, part : part + GROUP]
+                if h % 2 == 1:
+                    q = pltpu.roll(q, HALF, 1)
+                queries[rows, lo + part : lo + part + GROUP] = q.astype(jnp.bfloat16)
+        values[1, :AW, lo : lo + 256] = product[AW : 2 * AW].astype(jnp.bfloat16)
+        turned_atoms[:, lo : lo + 256] = product[2 * AW :].astype(jnp.bfloat16)
     for lo in range(128, ATOMS_DEV, 256):
         hi = min(lo + 256, ATOMS_DEV)
-        x = ext[lo:hi, :]
-        vt = lax.dot_general(both[AW:], x, NT, preferred_element_type=jnp.float32).astype(jnp.bfloat16)
-        values[0, :64, lo:hi] = vt[:64]
-        values[1, :64, lo:hi] = vt[64:]
-    for lo in range(0, ATOMS_DEV, 512):
-        x = ext[RIM + lo : RIM + lo + 512, :]
-        queries[:, lo : lo + 512] = lax.dot_general(
-            both[:AW], x, NT, preferred_element_type=jnp.float32
-        ).astype(jnp.bfloat16)
+        values[0, :AW, lo:hi] = dot_nt(value_t, ext[lo:hi, :]).astype(jnp.bfloat16)
+    pad = jnp.zeros((RIM, AW), jnp.bfloat16)
+    rest = jnp.concatenate([ext[ATOMS_DEV : ATOMS_DEV + RIM, :], pad], axis=0)
+    values[0, :AW, ATOMS_DEV:] = dot_nt(value_t, rest).astype(jnp.bfloat16)
 
     is_head = jnp.where(lax.rem(col, 8) == 0, 1, 0)
     is_leader = jnp.where(col == 0, 1, 0)
@@ -190,36 +244,26 @@
     for copy in halo:
         copy.start()
 
-    edge_low = jnp.where(me == 0, RIM, 0)
-    edge_high = jnp.where(me == DEVICES - 1, KEYS - RIM, KEYS)
-
-    def attend(g):
-        attend_group(g, edge_low, edge_high, off, keys, queries, values, att)
-
     for load in loads[3:]:
         load.wait()
-    eye = lax.broadcasted_iota(jnp.int32, (CZ, CZ), 0) == lax.broadcasted_iota(jnp.int32, (CZ, CZ), 1)
     for i in range(8):
-        base[:CZ, CZ * i : CZ * i + CZ] = jnp.where(eye, 1.0, 0.0).astype(jnp.bfloat16)
+        base[:CZ, CZ * i : CZ * i + CZ] = eye
+    w_out_t[...] = turned(w_out)
+    w_token_t[...] = turned(w_token)
     w_right[:CZ, :] = w_pair[CZ + CO : 2 * CZ + CO, :]
     for m in range(4):
         w_right[CZ + CO * m : CZ + CO * m + CO, :] = w_pair[2 * CZ + CO :, :]
 
-    for g in range(1, 6):
-        attend(g)
+    attend(range(1, 7), me, off, keys, queries, values, att)
 
     for copy in halo:
         copy.wait()
     for lo in (0, EXT - RIM):
         keys[lo : lo + RIM, :] = dot(ext[lo : lo + RIM, :], wk[...]).astype(jnp.bfloat16)
-    for lo in (0, EXT - 128):
-        vt = lax.dot_general(
-            both[AW:], ext[lo : lo + 128, :], NT, preferred_element_type=jnp.float32
-        ).astype(jnp.bfloat16)
-        values[0, :64, lo : lo + 128] = vt[:64]
-        values[1, :64, lo : lo + 128] = vt[64:]
-    attend(0)
-    attend(6)
+    values[0, :AW, :GROUP] = dot_nt(value_t, ext[:GROUP, :]).astype(jnp.bfloat16)
+    rest = jnp.concatenate([ext[EXT - RIM :, :], pad], axis=0)
+    values[1, :AW, ATOMS_DEV:] = dot_nt(value_t, rest).astype(jnp.bfloat16)
+    attend([0], me, off, keys, queries, values, att)
 
     lane = lax.broadcasted_iota(jnp.int32, (16, CZ), 1)
 
@@ -279,7 +323,7 @@
 
         return normed
 
-    hidden_rows(0, 896, ext, att, w_out, w_token, hid)
+    hidden_rows(0, 896, turned_atoms, att, w_out_t, w_token_t, hid)
     pooled = pooled_rows(-16, 80, 0, 896, me, token, hid)
     spill_out[...] = pooled[8:16]
     spill = pltpu.make_async_remote_copy(
@@ -305,11 +349,9 @@
         for r in range(1, ROWS):
             left_copy(left_all.at[r], (r, 0), r).start()
 
-    for g in range(7, 11):
-        attend(g)
-
-    attend(11)
-    hidden_rows(896, ATOMS_DEV, ext, att, w_out, w_token, hid)
+    attend(range(7, 12), me, off, keys, queries, values, att)
+
+    hidden_rows(896, ATOMS_DEV, turned_atoms, att, w_out_t, w_token_t, hid)
     pooled = pooled_rows(HALF, HALF, 768, ATOMS_DEV, me, token, hid)
     spill.wait()
     pooled = jnp.concatenate([pooled[:56], pooled[56:] + spill_in[...]], axis=0)
@@ -443,9 +485,12 @@
             pltpu.VMEM((EXT, AW), bf16),
             pltpu.VMEM((EXT, AW), bf16),
             pltpu.VMEM((AW, ATOMS_DEV), bf16),
-            pltpu.VMEM((2, 80, EXT), bf16),
-            pltpu.VMEM((ATOMS_DEV, AW), bf16),
-            pltpu.VMEM((ATOMS_DEV, WIDE), bf16),
+            pltpu.VMEM((2, AW + 16, EXT), bf16),
+            pltpu.VMEM((AW, ATOMS_DEV), bf16),
+            pltpu.VMEM((WIDE, ATOMS_DEV), bf16),
+            pltpu.VMEM((AW, ATOMS_DEV), bf16),
+            pltpu.VMEM((AW, AW), bf16),
+            pltpu.VMEM((TW, AW), bf16),
             pltpu.VMEM((2 * CZ, TW), bf16),
             pltpu.VMEM((8, WIDE), f32),
             pltpu.VMEM((8, WIDE), f32),

time: 31.3 us -> 30.9 us (0.987)
  Pallas kernels: 29.9 us -> 29.5 us
    pallas_call x1, Pallas kernels: 29.9 us -> 29.5 us  [body(): pl.pallas_call(embed_kernel, out_shape=pltpu.VMEM((8, ROWS * TOK_DEV, CZ)...]
where the time goes in v4:
time: 30.9 us; the launch traced here: 30.8 us
  Pallas kernels  29.5 us (95%)
  local copies, waits for them, and re-layouts  1.32 us (4%)
    pallas_call x1, Pallas kernels, body(): pl.pallas_call(embed_kernel, out_shape=pltpu.VMEM((8, ROWS * TOK_DEV, CZ)...  29.5 us
    unnamed x1, local copies, waits for them, and re-layouts  1.32 us

profile of v4, /device:TPU:65, one launch (start us, length us, event | category | flops | bytes accessed | tf_op | source)
XLA Modules:
  0.0 30.8 jit_solution(9110245946432732742)
XLA Ops:
  0.0 29.5 %embed.1 = bf16[8,1024,128]{2,1,0:T(8,128)(2,1)S(1)} custom-call(bf16[1536,128]{1,0:T(8,128)(2,1)} %atoms.1, s32[48]{0:T(128)} %off_hbm.1, s32[1536]{0:T(1024)} %token_hbm.1, bf16[128,128]{1,0:T(8,128)(2,1)} %wq_hbm.1, bf16[128,128]{1,0:T(8,128)(2,1)} %wk_hbm.1, bf16[128,128]{1,0:T(8,128)(2,1)} %wv_hbm.1, bf16[128,128]{1,0:T(8,128)(2,1)} %w_out_hbm.1, ...), custom_call_target="tpu_custom_call" | custom-call | tf_op jit(solution)/shard_map/embed/pallas_call | solution.py:467
  29.5 1.3 %copy.13 = bf16[8,1024,128]{2,1,0:T(8,128)(2,1)} copy(bf16[8,1024,128]{2,1,0:T(8,128)(2,1)S(1)} %embed.1) | data formatting | bytes 4194304

commit v5 on v4

v5 whole, which is shorter than its diff:
```python
import jax
import jax.numpy as jnp
from jax import lax
from jax.experimental import pallas as pl
from jax.experimental.pallas import tpu as pltpu
from jax.sharding import PartitionSpec as P

AW = 128
HEADS = 4
TW = 384
CZ = 128
CO = 32
QB = 32
RIM = 64
ROWS = 8
COLS = 32
DEVICES = ROWS * COLS
ATOMS_DEV = 1536
TOK_DEV = 128
NEXT = 128
NEXT_USED = 96
EXT = RIM + ATOMS_DEV + NEXT
WIDTH = ATOMS_DEV + NEXT
GROUP = 128
GROUPS = ATOMS_DEV // GROUP
UNITS = 2 * GROUPS
AHEAD = 3
BEHIND = 2
HALF = 64
EDGE = 16
TOKENS = (TOK_DEV - 2 * EDGE, 2 * EDGE)
BLOCK = (128, 48)
WIDE = TW + 128
EXP_SCALE = float(32 ** -0.5 * 1.4426950408889634)
MESH = pl.DeviceIdType.MESH
NT = (((1,), (1,)), ((), ()))


def dot(a, b):
    return jnp.dot(a, b, preferred_element_type=jnp.float32)


def place(device):
    return (lax.div(device, COLS), lax.rem(device, COLS))


def dot_nt(a, b):
    return lax.dot_general(a, b, NT, preferred_element_type=jnp.float32)


def turned(w):
    return w[...].astype(jnp.float32).T.astype(jnp.bfloat16)


def unit_scores(unit, keys, queries):
    g, j = unit // 2, unit % 2
    q = queries[:, GROUP * g : GROUP * g + GROUP]
    side = (lax.broadcasted_iota(jnp.int32, (HALF, GROUP), 0) // 32 == j) == (
        lax.broadcasted_iota(jnp.int32, (HALF, GROUP), 1) < HALF
    )
    none = jnp.zeros((HALF, GROUP), jnp.bfloat16)
    heads = [jnp.where(side, q[HALF * t : HALF * t + HALF], none) for t in range(2)]
    operand = jnp.concatenate(
        [jnp.concatenate([heads[0], none], axis=1), jnp.concatenate([none, heads[1]], axis=1)], axis=0
    )
    return dot(keys[HALF * unit : HALF * unit + 192, :], operand)


def unit_softmax(unit, scores, me, off, off_next):
    lane = lax.broadcasted_iota(jnp.int32, (1, GROUP), 1)
    second = lax.rem(lane // QB, 2) == 1
    if unit == UNITS:
        start = off_next[8:9, :].astype(jnp.int32) + RIM
    else:
        start = jnp.where(second, off[2 * unit + 1] + RIM + QB, off[2 * unit] + RIM)
    low, high = start, start + 128
    if unit == 0:
        low = jnp.maximum(low, jnp.where(me == 0, RIM, 0))
    if unit == UNITS - 1:
        high = jnp.minimum(high, jnp.where(me == DEVICES - 1, 128, 192))
    row = lax.broadcasted_iota(jnp.int32, (HALF, GROUP), 0)
    enters, stays = row >= low, row + 128 < high
    parts = []
    for t in range(2):
        tile = scores[:, GROUP * t : GROUP * t + GROUP]
        tile = jnp.concatenate(
            [jnp.where(enters, tile[:64], -1e30), tile[64:128], jnp.where(stays, tile[128:], -1e30)], axis=0
        )
        top = jnp.max(tile, axis=0, keepdims=True)
        parts.append(jnp.exp2((tile - top) * EXP_SCALE).astype(jnp.bfloat16))
    return jnp.concatenate(
        [jnp.concatenate(parts, axis=1), jnp.zeros((HALF, 2 * GROUP), jnp.bfloat16)], axis=0
    )


def group_store(g, mixed, att):
    left = lax.broadcasted_iota(jnp.int32, (1, GROUP), 1) < HALF
    for h in range(HEADS):
        lanes = slice(GROUP * (h // 2), GROUP * (h // 2) + GROUP)
        a, b = mixed if h % 2 == 0 else mixed[::-1]
        total = jnp.where(left, a[AW : AW + 1, lanes], b[AW : AW + 1, lanes])
        value = jnp.where(left, a[32 * h : 32 * h + 32, lanes], b[32 * h : 32 * h + 32, lanes]) * (1.0 / total)
        if h % 2 == 1:
            value = pltpu.roll(value, HALF, 1)
        att[32 * h : 32 * h + 32, GROUP * g : GROUP * g + GROUP] = value.astype(jnp.bfloat16)


def attend(units, me, off, off_next, keys, queries, values, att, mixed):
    scores, lifted = {}, {}
    for i in range(len(units) + AHEAD + BEHIND):
        if i < len(units):
            scores[i] = unit_scores(units[i], keys, queries)
        k = i - AHEAD
        if 0 <= k < len(units):
            lifted[k] = unit_softmax(units[k], scores.pop(k), me, off, off_next)
        k = i - AHEAD - BEHIND
        if 0 <= k < len(units):
            g, j = units[k] // 2, units[k] % 2
            mixed[units[k]] = dot(values[j, :, GROUP * g : GROUP * g + 2 * GROUP], lifted.pop(k))
            if units[k] == UNITS:
                mixed[UNITS + 1] = mixed[UNITS]
            if 2 * g in mixed and 2 * g + 1 in mixed:
                group_store(g, [mixed.pop(2 * g), mixed.pop(2 * g + 1)], att)


def hidden_rows(lo, hi, turned_atoms, att, w_out_t, w_token_t, hid):
    mixed = dot(w_out_t[...], att[:, lo:hi])
    update = (turned_atoms[:, lo:hi].astype(jnp.float32) + mixed).astype(jnp.bfloat16)
    hid[:TW, lo:hi] = jnp.maximum(dot(w_token_t[...], update), 0.0).astype(jnp.bfloat16)


def pooled_rows(first, count, lo, hi, device, token, hid, flags=None):
    slot = token[...].reshape(1, ATOMS_DEV)[:, lo:hi] - device * TOK_DEV
    rows = lax.broadcasted_iota(jnp.int32, (count, hi - lo), 0) + first
    one_hot = jnp.where(rows == slot, 1.0, 0.0).astype(jnp.bfloat16)
    if flags is not None:
        last = lax.broadcasted_iota(jnp.int32, (count, NEXT), 0) == count - 1
        one_hot = jnp.concatenate([one_hot, jnp.where(last, flags, 0.0).astype(jnp.bfloat16)], axis=1)
        hi += NEXT
    return dot_nt(one_hot, hid[:, lo:hi])


def token_normed(pooled, gain):
    count = pooled[:, TW:]
    single = pooled[:, :TW] / jnp.concatenate([count] * 3, axis=1)
    centre = single - jnp.mean(single, axis=1, keepdims=True)
    variance = jnp.mean(centre * centre, axis=1, keepdims=True)
    return (centre * lax.rsqrt(variance + 1e-05) * gain).astype(jnp.bfloat16)


def embed_kernel(
    atoms, off_hbm, token_hbm, wq_hbm, wk_hbm, wv_hbm, w_out_hbm, w_token_hbm, gain_hbm, w_pair_hbm, w_outer_hbm,
    result,
    off, token, wq, wk, wv, w_out, w_token, gain, w_pair, w_outer,
    gathered_inner, gathered_outer, base,
    ext, keys, queries, values, att, hid, turned_atoms, w_out_t, w_token_t, w_right,
    note_out, note_in, block_inner, block_outer, left_all, left_in,
    own_sem, load_sem, halo_send, halo_recv,
    first_send, first_recv, local_sem, pass_send, pass_recv, left_send, left_recv, far_ready, left_ready,
):
    gathered, block = (gathered_inner, gathered_outer), (block_inner, block_outer)
    row = lax.axis_index("row")
    col = lax.axis_index("col")
    me = row * COLS + col
    before = lax.rem(me + DEVICES - 1, DEVICES)
    after = lax.rem(me + 1, DEVICES)
    slot = lax.rem(me, ROWS)
    my_y, my_z = lax.div(row, 2), lax.rem(row, 2)
    my_x, my_zh = lax.div(col, 8), lax.rem(lax.div(col, 2), 4)
    depth = 2 * my_zh + my_z
    group_col = lax.div(me, ROWS)
    relay_y = lax.rem(my_y + 6 + my_zh - 2 * my_z - lax.div(my_x, 2), 4)
    targets = [(2 * relay_y + i) * COLS + group_col for i in range(2)]
    target_depth = [4 * my_z + 2 * lax.div(my_x, 2) + i for i in range(2)]

    def held_by(y):
        return 2 * lax.rem(y + 6 + my_zh - my_x, 4)

    held = held_by(my_y)
    sources = [ROWS * col + held + k for k in range(2)]
    source_depth = held + lax.div(my_zh, 2)
    keeps = jnp.where((targets[0] == me) | (targets[1] == me), 1, 0)
    col_in = lax.rem(col, 8)
    is_head, is_leader, is_first, is_last = col_in == 1, col == 1, me == 0, me == DEVICES - 1
    parent = jnp.where(is_leader, 0, jnp.where(is_head, row * COLS + 1, me - col_in + 1))

    def count(condition):
        return jnp.where(condition, 1, 0)

    def signal(device, semaphore=None):
        pl.semaphore_signal(
            barrier if semaphore is None else semaphore, inc=1, device_id=place(device), device_id_type=MESH
        )

    barrier = pltpu.get_barrier_semaphore()

    @pl.when(jnp.logical_not(is_first))
    def _():
        signal(before)

    @pl.when(jnp.logical_not(is_last))
    def _():
        signal(after)

    @pl.when(is_head)
    def _():
        signal(parent)

    arrivals = 2 + 3 - count(is_first) - count(is_last) + 8 * count(is_first) + 3 * count(is_leader)
    for k in range(2):
        @pl.when((sources[k] != me) & (source_depth >= depth))
        def _():
            signal(sources[k])

        arrivals += count((sources[k] != me) & (source_depth < depth))
    for i in range(2):
        @pl.when((targets[i] != me) & (target_depth[i] > depth))
        def _():
            signal(targets[i])

        arrivals += count((targets[i] != me) & (target_depth[i] <= depth))
    late_targets = sum(count((targets[i] != me) & (target_depth[i] > depth)) for i in range(2))
    for i in range(1, 4):
        signal((2 * lax.rem(my_y + i, 4) + my_z) * COLS + col)
    child = jnp.logical_not(is_head | is_first)
    arrivals += count(child)
    children = 7 - count((row == 0) & is_leader)

    def each_child(act):
        for c in range(8):
            if c != 1:
                @pl.when(is_head & (me + c != 1))
                def _():
                    act(me + c - 1, 16 + c)

    def each_leader(act):
        @pl.when(is_first)
        def _():
            for r in range(ROWS):
                act(r * COLS + 1, r)

    def each_head(act):
        @pl.when(is_leader)
        def _():
            for x in range(1, 4):
                act(me + 8 * x, 8 + x)

    each_child(lambda to, _: signal(to))

    own = pltpu.make_async_copy(atoms, ext.at[pl.ds(RIM, ATOMS_DEV)], own_sem)
    own.start()
    pieces = [
        (wq_hbm, wq), (wk_hbm, wk), (wv_hbm, wv), (off_hbm, off), (w_out_hbm, w_out),
        (token_hbm, token), (w_token_hbm, w_token), (gain_hbm, gain), (w_pair_hbm, w_pair),
        (w_outer_hbm, w_outer),
    ]
    loads = [pltpu.make_async_copy(a, b, load_sem.at[i]) for i, (a, b) in enumerate(pieces)]
    for load in loads:
        load.start()
    for load in loads[:3]:
        load.wait()

    one = lax.broadcasted_iota(jnp.int32, (CZ, CZ), 0) == lax.broadcasted_iota(jnp.int32, (CZ, CZ), 1)
    eye = jnp.where(one, 1.0, 0.0).astype(jnp.bfloat16)
    value_t = turned(wv)
    left_side = jnp.concatenate([turned(wq), value_t, eye], axis=0)
    hid[TW:, :] = jnp.ones((WIDE - TW, WIDTH), jnp.bfloat16)
    for j in range(2):
        values[j, AW:, :] = jnp.ones((16, WIDTH + GROUP), jnp.bfloat16)
    own.wait()
    for lo in range(0, ATOMS_DEV, 512):
        x = ext[RIM + lo : RIM + lo + 512, :]
        keys[RIM + lo : RIM + lo + 512, :] = dot(x, wk[...]).astype(jnp.bfloat16)
    def keep_product(lo, size, product):
        for h in range(HEADS):
            rows = slice(32 * h, 32 * h + 32)
            for part in range(0, size, GROUP):
                q = product[rows, part : part + GROUP]
                if h % 2 == 1:
                    q = pltpu.roll(q, HALF, 1)
                queries[rows, lo + part : lo + part + GROUP] = q.astype(jnp.bfloat16)
        values[1, :AW, lo : lo + size] = product[AW : 2 * AW].astype(jnp.bfloat16)
        turned_atoms[:, lo : lo + size] = product[2 * AW :].astype(jnp.bfloat16)

    for lo in range(0, ATOMS_DEV, 256):
        keep_product(lo, 256, dot_nt(left_side, ext[RIM + lo : RIM + lo + 256, :]))
    for lo in range(128, ATOMS_DEV, 256):
        hi = min(lo + 256, ATOMS_DEV)
        values[0, :AW, lo:hi] = dot_nt(value_t, ext[lo:hi, :]).astype(jnp.bfloat16)
    pad = jnp.zeros((RIM, AW), jnp.bfloat16)
    rest = jnp.concatenate([ext[ATOMS_DEV : ATOMS_DEV + RIM, :], pad], axis=0)
    values[0, :AW, ATOMS_DEV : ATOMS_DEV + GROUP] = dot_nt(value_t, rest).astype(jnp.bfloat16)

    for load in loads[3:]:
        load.wait()
    flags = token[...].reshape(1, ATOMS_DEV)[:, :NEXT] == me * TOK_DEV - 1
    upper = lax.broadcasted_iota(jnp.int32, (16, NEXT), 0) < 8
    note = jnp.where(upper, jnp.where(flags, 1.0, 0.0), off[0].astype(jnp.float32))
    note_out[...] = note.astype(jnp.bfloat16)
    ext[RIM + ATOMS_DEV + NEXT_USED :, :] = jnp.zeros((NEXT - NEXT_USED, AW), jnp.bfloat16)

    @pl.when(is_first)
    def _():
        ext[:RIM, :] = jnp.zeros((RIM, AW), jnp.bfloat16)

    @pl.when(is_last)
    def _():
        ext[RIM + ATOMS_DEV :, :] = jnp.zeros((NEXT, AW), jnp.bfloat16)
        note_in[...] = jnp.zeros((16, NEXT), jnp.bfloat16)

    pl.semaphore_wait(barrier, arrivals)
    for k in range(2):
        @pl.when((sources[k] != me) & (source_depth < depth))
        def _():
            signal(sources[k], far_ready)

    @pl.when(child)
    def _():
        signal(parent, left_ready)

    to_after = pltpu.make_async_remote_copy(
        src_ref=atoms.at[pl.ds(ATOMS_DEV - RIM, RIM)], dst_ref=ext.at[pl.ds(0, RIM)],
        send_sem=halo_send.at[0], recv_sem=halo_recv.at[0],
        device_id=place(after), device_id_type=MESH,
    )
    to_before = [
        pltpu.make_async_remote_copy(
            src_ref=atoms.at[pl.ds(0, NEXT_USED)], dst_ref=ext.at[pl.ds(RIM + ATOMS_DEV, NEXT_USED)],
            send_sem=halo_send.at[1], recv_sem=halo_recv.at[1],
            device_id=place(before), device_id_type=MESH,
        ),
        pltpu.make_async_remote_copy(
            src_ref=note_out, dst_ref=note_in, send_sem=halo_send.at[2], recv_sem=halo_recv.at[2],
            device_id=place(before), device_id_type=MESH,
        ),
    ]

    @pl.when(jnp.logical_not(is_last))
    def _():
        to_after.start()

    @pl.when(jnp.logical_not(is_first))
    def _():
        for copy in to_before:
            copy.start()

    for i in range(8):
        base[:CZ, CZ * i : CZ * i + CZ] = eye
    w_out_t[...] = turned(w_out)
    w_token_t[...] = turned(w_token)
    w_right[:CZ, :] = w_pair[CZ + CO : 2 * CZ + CO, :]
    for m in range(4):
        w_right[CZ + CO * m : CZ + CO * m + CO, :] = w_pair[2 * CZ + CO :, :]

    mixed = {}
    attend(list(range(1, UNITS - 1)), me, off, note_in, keys, queries, values, att, mixed)

    def first_copy(part, i):
        return pltpu.make_async_remote_copy(
            src_ref=block[part], dst_ref=gathered[part].at[slot],
            send_sem=first_send.at[part, i], recv_sem=first_recv.at[part, lax.rem(slot, 2)],
            device_id=place(targets[i]), device_id_type=MESH,
        )

    def local_copy(part):
        return pltpu.make_async_copy(block[part], gathered[part].at[slot], local_sem.at[part])

    def first_sends(part):
        for i in range(2):
            @pl.when(targets[i] != me)
            def _():
                first_copy(part, i).start()

        @pl.when(keeps == 1)
        def _():
            local_copy(part).start()

    def pass_copy(part, i, start):
        return pltpu.make_async_remote_copy(
            src_ref=gathered[part].at[pl.ds(start, 2)], dst_ref=gathered[part].at[pl.ds(start, 2)],
            send_sem=pass_send.at[part, i], recv_sem=pass_recv.at[part, i],
            device_id=(2 * lax.rem(my_y + i, 4) + my_z, col), device_id_type=MESH,
        )

    def pass_on(part):
        for k in range(2):
            @pl.when(sources[k] != me)
            def _():
                pltpu.make_async_remote_copy(
                    src_ref=block[part], dst_ref=gathered[part].at[held + k],
                    send_sem=first_send.at[part, 0], recv_sem=first_recv.at[part, k],
                    device_id=place(sources[k]), device_id_type=MESH,
                ).wait_recv()

        @pl.when(keeps == 1)
        def _():
            local_copy(part).wait()

        for i in range(1, 4):
            pass_copy(part, i, held).start()

    def finish(part, pooled):
        tokens = TOKENS[part]
        normed = token_normed(pooled, gain[...].reshape(1, TW).astype(jnp.float32))
        right = dot_nt(normed, w_right[...])
        quarter = tokens // 4
        lane = lax.broadcasted_iota(jnp.int32, (quarter, CZ), 1)
        packed = right[:quarter, CZ:]
        for m in range(1, 4):
            packed = jnp.where(lane // CO == m, right[quarter * m : quarter * m + quarter, CZ:], packed)
        empty = jnp.zeros((BLOCK[part] - tokens - quarter, CZ), jnp.float32)
        block[part][:tokens, :] = right[:, :CZ].astype(jnp.bfloat16)
        block[part][tokens:, :] = jnp.concatenate([packed, empty], axis=0).astype(jnp.bfloat16)
        return normed

    hidden_rows(GROUP, ATOMS_DEV - GROUP, turned_atoms, att, w_out_t, w_token_t, hid)
    pooled = pooled_rows(EDGE, TOKENS[0], GROUP, ATOMS_DEV - GROUP, me, token, hid)
    inner = finish(0, pooled)

    @pl.when(late_targets == 0)
    def _():
        first_sends(0)

    @pl.when(jnp.logical_not(is_last))
    def _():
        for copy in to_before:
            copy.wait_recv()

    @pl.when(jnp.logical_not(is_first))
    def _():
        to_after.wait_recv()

    keys[:RIM, :] = dot(ext[:RIM, :], wk[...]).astype(jnp.bfloat16)
    values[0, :AW, :GROUP] = dot_nt(value_t, ext[:GROUP, :]).astype(jnp.bfloat16)
    x = ext[RIM + ATOMS_DEV :, :]
    keys[RIM + ATOMS_DEV :, :] = dot(x, wk[...]).astype(jnp.bfloat16)
    keep_product(ATOMS_DEV, NEXT, dot_nt(left_side, x))
    rest = jnp.concatenate([ext[ATOMS_DEV:, :], pad], axis=0)
    values[0, :AW, ATOMS_DEV:] = dot_nt(value_t, rest).astype(jnp.bfloat16)
    attend([0, UNITS, UNITS - 1], me, off, note_in, keys, queries, values, att, mixed)

    hidden_rows(0, GROUP, turned_atoms, att, w_out_t, w_token_t, hid)
    hidden_rows(ATOMS_DEV - GROUP, WIDTH, turned_atoms, att, w_out_t, w_token_t, hid)
    low = pooled_rows(0, EDGE, 0, 256, me, token, hid)
    flags = note_in[:1, :].astype(jnp.float32)
    high = pooled_rows(TOK_DEV - EDGE, EDGE, ATOMS_DEV - 256, ATOMS_DEV, me, token, hid, flags)
    outer = finish(1, jnp.concatenate([low, high], axis=0))

    @pl.when(late_targets == 0)
    def _():
        first_sends(1)

    def left_copy(source, to, index):
        return pltpu.make_async_remote_copy(
            src_ref=source, dst_ref=left_in, send_sem=left_send.at[index], recv_sem=left_recv,
            device_id=place(to), device_id_type=MESH,
        )

    def left_to(child, index):
        return left_copy(left_all.at[index] if index < ROWS else left_in, child, index)

    @pl.when(is_first)
    def _():
        normed = jnp.concatenate([outer[:EDGE], inner[: HALF - EDGE]], axis=0)
        left = dot_nt(normed, w_pair[: 2 * CZ, :])
        for r in range(ROWS):
            rows = left[8 * r : 8 * r + 8]
            left_all[r] = jnp.concatenate([rows[:, :CZ], rows[:, CZ:]], axis=0).astype(jnp.bfloat16)
        left_in[...] = left_all[0]

    each_leader(lambda to, index: left_to(to, index).start())

    @pl.when(is_leader)
    def _():
        left_copy(left_in, parent, 0).wait_recv()

    each_head(lambda to, index: left_to(to, index).start())

    @pl.when(late_targets != 0)
    def _():
        pl.semaphore_wait(far_ready, late_targets)
        first_sends(0)
        first_sends(1)

    @pl.when(is_head & jnp.logical_not(is_leader))
    def _():
        left_copy(left_in, parent, 0).wait_recv()

    @pl.when(is_head)
    def _():
        pl.semaphore_wait(left_ready, children)

    each_child(lambda to, index: left_to(to, index).start())
    pass_on(0)
    pass_on(1)

    @pl.when(child)
    def _():
        left_copy(left_in, parent, 0).wait_recv()

    mix_left(left_in, w_outer, base)
    left = left_in[:8, :].astype(jnp.float32)

    def arrived(part):
        for i in range(1, 4):
            theirs = held_by(my_y + 4 - i)
            pass_copy(part, i, theirs).wait_recv()
            pair_block(gathered[part], part, theirs, base, left, result)

    pair_block(gathered[0], 0, held, base, left, result)
    arrived(0)
    pair_block(gathered[1], 1, held, base, left, result)
    arrived(1)

    for each in (each_leader, each_head, each_child):
        each(lambda to, index: left_to(to, index).wait_send())

    @pl.when(jnp.logical_not(is_last))
    def _():
        to_after.wait_send()

    @pl.when(jnp.logical_not(is_first))
    def _():
        for copy in to_before:
            copy.wait_send()

    for part in range(2):
        for i in range(1, 4):
            pass_copy(part, i, held).wait_send()
        for i in range(2):
            @pl.when(targets[i] != me)
            def _():
                first_copy(part, i).wait_send()


def mix_left(left_in, w_outer, base):
    outer = left_in[8:, :CO]
    spread = lax.broadcasted_iota(jnp.int32, (CO, CO * CO), 1) // CO
    spread = jnp.where(spread == lax.broadcasted_iota(jnp.int32, (CO, CO * CO), 0), 1.0, 0.0)
    wide = dot(outer, spread.astype(jnp.bfloat16))
    n = lax.broadcasted_iota(jnp.int32, (CO, CO * CO), 0)
    mine = lax.rem(lax.broadcasted_iota(jnp.int32, (CO, CO * CO), 1), CO) == n
    expanded = [jnp.where(mine, wide[i : i + 1], 0.0).astype(jnp.bfloat16) for i in range(8)]
    mixing = dot(jnp.concatenate(expanded, axis=0), w_outer[...]).astype(jnp.bfloat16)
    for i in range(8):
        for k in range(4):
            base[CZ + CO * k : CZ + CO * k + CO, CZ * i : CZ * i + CZ] = mixing[CO * i : CO * i + CO]


def pair_block(gathered, part, start, base, left, result):
    tokens, quarter = TOKENS[part], TOKENS[part] // 4
    lane = lax.broadcasted_iota(jnp.int32, (quarter, CZ), 1)
    pieces = []
    for k in range(2):
        packed = gathered[start + k, tokens:, :].astype(jnp.float32)[:quarter]
        outer = [jnp.where(lane // CO == m, packed, 0.0) for m in range(4)]
        outer = jnp.concatenate(outer, axis=0).astype(jnp.bfloat16)
        pieces.append(jnp.concatenate([gathered[start + k, :tokens, :], outer], axis=1))
    rows = jnp.concatenate(pieces, axis=0)
    spans = [(0, EDGE, tokens)] if part == 0 else [(0, 0, EDGE), (EDGE, TOK_DEV - EDGE, EDGE)]
    for i in range(0, 8, 2):
        grid = dot(rows, base[:, CZ * i : CZ * i + 2 * CZ])
        for j in range(2):
            total = (grid[:, CZ * j : CZ * j + CZ] + left[i + j : i + j + 1]).astype(jnp.bfloat16)
            for k in range(2):
                for first, to, size in spans:
                    target = pl.multiple_of(TOK_DEV * (start + k) + to, EDGE)
                    result[i + j, pl.ds(target, size), :] = total[tokens * k + first : tokens * k + first + size]


def body(
    atoms, window_offsets, atom_token, w_query, w_key, w_value, w_out, w_token, gain_token, w_pair, w_outer
):
    hbm = pl.BlockSpec(memory_space=pltpu.HBM)
    dma = pltpu.SemaphoreType.DMA
    bf16 = jnp.bfloat16
    return pl.pallas_call(
        embed_kernel,
        out_shape=pltpu.VMEM((8, ROWS * TOK_DEV, CZ), bf16),
        in_specs=[hbm] * 11,
        out_specs=pl.BlockSpec(memory_space=pltpu.VMEM),
        scratch_shapes=[
            pltpu.SMEM((ATOMS_DEV // QB,), jnp.int32),
            pltpu.VMEM((ATOMS_DEV,), jnp.int32),
            pltpu.VMEM((AW, AW), bf16),
            pltpu.VMEM((AW, AW), bf16),
            pltpu.VMEM((AW, AW), bf16),
            pltpu.VMEM((AW, AW), bf16),
            pltpu.VMEM((AW, TW), bf16),
            pltpu.VMEM((TW,), bf16),
            pltpu.VMEM((2 * CZ + 2 * CO, TW), bf16),
            pltpu.VMEM((CO * CO, CZ), bf16),
            pltpu.VMEM((ROWS, BLOCK[0], CZ), bf16),
            pltpu.VMEM((ROWS, BLOCK[1], CZ), bf16),
            pltpu.VMEM((2 * CZ, 8 * CZ), bf16),
            pltpu.VMEM((EXT, AW), bf16),
            pltpu.VMEM((EXT, AW), bf16),
            pltpu.VMEM((AW, WIDTH), bf16),
            pltpu.VMEM((2, AW + 16, WIDTH + GROUP), bf16),
            pltpu.VMEM((AW, WIDTH), bf16),
            pltpu.VMEM((WIDE, WIDTH), bf16),
            pltpu.VMEM((AW, WIDTH), bf16),
            pltpu.VMEM((AW, AW), bf16),
            pltpu.VMEM((TW, AW), bf16),
            pltpu.VMEM((2 * CZ, TW), bf16),
            pltpu.VMEM((16, NEXT), bf16),
            pltpu.VMEM((16, NEXT), bf16),
            pltpu.VMEM((BLOCK[0], CZ), bf16),
            pltpu.VMEM((BLOCK[1], CZ), bf16),
            pltpu.VMEM((ROWS, 16, CZ), bf16),
            pltpu.VMEM((16, CZ), bf16),
            dma, dma((10,)), dma((3,)), dma((3,)),
            dma((2, 2)), dma((2, 2)), dma((2,)), dma((2, 4)), dma((2, 4)), dma((COLS,)), dma,
            pltpu.SemaphoreType.REGULAR, pltpu.SemaphoreType.REGULAR,
        ],
        compiler_params=pltpu.CompilerParams(
            collective_id=0, has_side_effects=True, vmem_limit_bytes=60 * 1024 * 1024
        ),
        name="embed",
    )(
        atoms, window_offsets, atom_token, w_query, w_key, w_value, w_out, w_token, gain_token, w_pair.T,
        w_outer,
    )


def solution(mesh):
    split = P(("row", "col"))
    placed = (P(("row", "col"), None), split, split) + (P(),) * 8
    return jax.shard_map(
        body, mesh=mesh, in_specs=placed, out_specs=P("row", "col", None), check_vma=False
    )
```

time: 30.9 us -> 30 us (0.971)
  Pallas kernels: 29.5 us -> 28.5 us
    pallas_call x1, Pallas kernels: 29.5 us -> 28.5 us  [body(): pl.pallas_call(embed_kernel, out_shape=pltpu.VMEM((8, ROWS * TOK_DEV, CZ)...]
where the time goes in v5:
time: 30 us; the launch traced here: 29.9 us
  Pallas kernels  28.5 us (95%)
  local copies, waits for them, and re-layouts  1.32 us (4%)
    pallas_call x1, Pallas kernels, body(): pl.pallas_call(embed_kernel, out_shape=pltpu.VMEM((8, ROWS * TOK_DEV, CZ)...  28.5 us
    unnamed x1, local copies, waits for them, and re-layouts  1.32 us

profile of v5, /device:TPU:65, one launch (start us, length us, event | category | flops | bytes accessed | tf_op | source)
XLA Modules:
  0.0 29.9 jit_solution(6344703427424181037)
XLA Ops:
  0.0 28.5 %embed.1 = bf16[8,1024,128]{2,1,0:T(8,128)(2,1)S(1)} custom-call(bf16[1536,128]{1,0:T(8,128)(2,1)} %atoms.1, s32[48]{0:T(128)} %off_hbm.1, s32[1536]{0:T(1024)} %token_hbm.1, bf16[128,128]{1,0:T(8,128)(2,1)} %wq_hbm.1, bf16[128,128]{1,0:T(8,128)(2,1)} %wk_hbm.1, bf16[128,128]{1,0:T(8,128)(2,1)} %wv_hbm.1, bf16[128,128]{1,0:T(8,128)(2,1)} %w_out_hbm.1, ...), custom_call_target="tpu_custom_call" | custom-call | tf_op jit(solution)/shard_map/embed/pallas_call | solution.py:577
  28.6 1.3 %copy.13 = bf16[8,1024,128]{2,1,0:T(8,128)(2,1)} copy(bf16[8,1024,128]{2,1,0:T(8,128)(2,1)S(1)} %embed.1) | data formatting | bytes 4194304

commit v6 on v5

--- a/solution.py
+++ b/solution.py
@@ -28,8 +28,10 @@
 BEHIND = 2
 HALF = 64
 EDGE = 16
-TOKENS = (TOK_DEV - 2 * EDGE, 2 * EDGE)
-BLOCK = (128, 48)
+INNER = ((UNITS - 2, 128, 1408, 16, 96, 128, 1408),)
+TOKENS = tuple(piece[4] for piece in INNER) + (32,)
+PARTS = len(TOKENS)
+SPANS = tuple(((0, piece[3], piece[4]),) for piece in INNER) + (((0, 0, 16), (16, 112, 16)),)
 WIDE = TW + 128
 EXP_SCALE = float(32 ** -0.5 * 1.4426950408889634)
 MESH = pl.DeviceIdType.MESH
@@ -121,6 +123,7 @@
                 mixed[UNITS + 1] = mixed[UNITS]
             if 2 * g in mixed and 2 * g + 1 in mixed:
                 group_store(g, [mixed.pop(2 * g), mixed.pop(2 * g + 1)], att)
+            yield units[k]
 
 
 def hidden_rows(lo, hi, turned_atoms, att, w_out_t, w_token_t, hid):
@@ -152,13 +155,13 @@
     atoms, off_hbm, token_hbm, wq_hbm, wk_hbm, wv_hbm, w_out_hbm, w_token_hbm, gain_hbm, w_pair_hbm, w_outer_hbm,
     result,
     off, token, wq, wk, wv, w_out, w_token, gain, w_pair, w_outer,
-    gathered_inner, gathered_outer, base,
+    gathered0, gathered1, base,
     ext, keys, queries, values, att, hid, turned_atoms, w_out_t, w_token_t, w_right,
-    note_out, note_in, block_inner, block_outer, left_all, left_in,
+    note_out, note_in, block0, block1, left_all, left_in,
     own_sem, load_sem, halo_send, halo_recv,
     first_send, first_recv, local_sem, pass_send, pass_recv, left_send, left_recv, far_ready, left_ready,
 ):
-    gathered, block = (gathered_inner, gathered_outer), (block_inner, block_outer)
+    gathered, block = (gathered0, gathered1), (block0, block1)
     row = lax.axis_index("row")
     col = lax.axis_index("col")
     me = row * COLS + col
@@ -170,16 +173,18 @@
     depth = 2 * my_zh + my_z
     group_col = lax.div(me, ROWS)
     relay_y = lax.rem(my_y + 6 + my_zh - 2 * my_z - lax.div(my_x, 2), 4)
-    targets = [(2 * relay_y + i) * COLS + group_col for i in range(2)]
-    target_depth = [4 * my_z + 2 * lax.div(my_x, 2) + i for i in range(2)]
-
-    def held_by(y):
-        return 2 * lax.rem(y + 6 + my_zh - my_x, 4)
-
-    held = held_by(my_y)
-    sources = [ROWS * col + held + k for k in range(2)]
-    source_depth = held + lax.div(my_zh, 2)
-    keeps = jnp.where((targets[0] == me) | (targets[1] == me), 1, 0)
+    my_core = lax.rem(col, 2)
+    target = (2 * relay_y + my_core) * COLS + group_col
+    target_depth = 4 * my_z + 2 * lax.div(my_x, 2) + my_core
+
+    def held_by(y, z):
+        return 2 * lax.rem(y + 6 + my_zh - my_x, 4) + z
+
+    held = held_by(my_y, my_z)
+    source = ROWS * col + held
+    source_depth = 2 * lax.div(held, 2) + lax.div(my_zh, 2)
+    keeps = target == me
+    peers = [(i, j) for i in range(4) for j in range(2) if i + j > 0]
     col_in = lax.rem(col, 8)
     is_head, is_leader, is_first, is_last = col_in == 1, col == 1, me == 0, me == DEVICES - 1
     parent = jnp.where(is_leader, 0, jnp.where(is_head, row * COLS + 1, me - col_in + 1))
@@ -191,61 +196,6 @@
         pl.semaphore_signal(
             barrier if semaphore is None else semaphore, inc=1, device_id=place(device), device_id_type=MESH
         )
-
-    barrier = pltpu.get_barrier_semaphore()
-
-    @pl.when(jnp.logical_not(is_first))
-    def _():
-        signal(before)
-
-    @pl.when(jnp.logical_not(is_last))
-    def _():
-        signal(after)
-
-    @pl.when(is_head)
-    def _():
-        signal(parent)
-
-    arrivals = 2 + 3 - count(is_first) - count(is_last) + 8 * count(is_first) + 3 * count(is_leader)
-    for k in range(2):
-        @pl.when((sources[k] != me) & (source_depth >= depth))
-        def _():
-            signal(sources[k])
-
-        arrivals += count((sources[k] != me) & (source_depth < depth))
-    for i in range(2):
-        @pl.when((targets[i] != me) & (target_depth[i] > depth))
-        def _():
-            signal(targets[i])
-
-        arrivals += count((targets[i] != me) & (target_depth[i] <= depth))
-    late_targets = sum(count((targets[i] != me) & (target_depth[i] > depth)) for i in range(2))
-    for i in range(1, 4):
-        signal((2 * lax.rem(my_y + i, 4) + my_z) * COLS + col)
-    child = jnp.logical_not(is_head | is_first)
-    arrivals += count(child)
-    children = 7 - count((row == 0) & is_leader)
-
-    def each_child(act):
-        for c in range(8):
-            if c != 1:
-                @pl.when(is_head & (me + c != 1))
-                def _():
-                    act(me + c - 1, 16 + c)
-
-    def each_leader(act):
-        @pl.when(is_first)
-        def _():
-            for r in range(ROWS):
-                act(r * COLS + 1, r)
-
-    def each_head(act):
-        @pl.when(is_leader)
-        def _():
-            for x in range(1, 4):
-                act(me + 8 * x, 8 + x)
-
-    each_child(lambda to, _: signal(to))
 
     own = pltpu.make_async_copy(atoms, ext.at[pl.ds(RIM, ATOMS_DEV)], own_sem)
     own.start()
@@ -257,6 +207,66 @@
     loads = [pltpu.make_async_copy(a, b, load_sem.at[i]) for i, (a, b) in enumerate(pieces)]
     for load in loads:
         load.start()
+
+    barrier = pltpu.get_barrier_semaphore()
+
+    @pl.when(jnp.logical_not(is_first))
+    def _():
+        signal(before)
+
+    @pl.when(jnp.logical_not(is_last))
+    def _():
+        signal(after)
+
+    @pl.when(is_head)
+    def _():
+        signal(parent)
+
+    arrivals = 2 - count(is_first) - count(is_last) + 8 * count(is_first) + 3 * count(is_leader)
+
+    @pl.when((source != me) & (source_depth >= depth))
+    def _():
+        signal(source)
+
+    @pl.when(jnp.logical_not(keeps) & (target_depth > depth))
+    def _():
+        signal(target)
+
+    arrivals += count((source != me) & (source_depth < depth))
+    arrivals += count(jnp.logical_not(keeps) & (target_depth <= depth))
+    late_target = jnp.logical_not(keeps) & (target_depth > depth)
+
+    def peer(i, j):
+        return (2 * lax.rem(my_y + i, 4) + lax.rem(my_z + j, 2)) * COLS + col
+
+    for i, j in peers:
+        signal(peer(i, j))
+    arrivals += len(peers)
+    child = jnp.logical_not(is_head | is_first)
+    arrivals += count(child)
+    children = 7 - count((row == 0) & is_leader)
+
+    def each_child(act):
+        for c in range(8):
+            if c != 1:
+                @pl.when(is_head & (me + c != 1))
+                def _():
+                    act(me + c - 1, 16 + c)
+
+    def each_leader(act):
+        @pl.when(is_first)
+        def _():
+            for r in range(ROWS):
+                act(r * COLS + 1, r)
+
+    def each_head(act):
+        @pl.when(is_leader)
+        def _():
+            for x in range(1, 4):
+                act(me + 8 * x, 8 + x)
+
+    each_child(lambda to, _: signal(to))
+
     for load in loads[:3]:
         load.wait()
 
@@ -309,10 +319,10 @@
         note_in[...] = jnp.zeros((16, NEXT), jnp.bfloat16)
 
     pl.semaphore_wait(barrier, arrivals)
-    for k in range(2):
-        @pl.when((sources[k] != me) & (source_depth < depth))
-        def _():
-            signal(sources[k], far_ready)
+
+    @pl.when((source != me) & (source_depth < depth))
+    def _():
+        signal(source, far_ready)
 
     @pl.when(child)
     def _():
@@ -353,73 +363,80 @@
         w_right[CZ + CO * m : CZ + CO * m + CO, :] = w_pair[2 * CZ + CO :, :]
 
     mixed = {}
-    attend(list(range(1, UNITS - 1)), me, off, note_in, keys, queries, values, att, mixed)
-
-    def first_copy(part, i):
+    inner_units = attend(list(range(1, UNITS - 1)), me, off, note_in, keys, queries, values, att, mixed)
+
+    def first_copy(part):
         return pltpu.make_async_remote_copy(
             src_ref=block[part], dst_ref=gathered[part].at[slot],
-            send_sem=first_send.at[part, i], recv_sem=first_recv.at[part, lax.rem(slot, 2)],
-            device_id=place(targets[i]), device_id_type=MESH,
+            send_sem=first_send.at[part], recv_sem=first_recv.at[part],
+            device_id=place(target), device_id_type=MESH,
         )
 
     def local_copy(part):
         return pltpu.make_async_copy(block[part], gathered[part].at[slot], local_sem.at[part])
 
     def first_sends(part):
-        for i in range(2):
-            @pl.when(targets[i] != me)
-            def _():
-                first_copy(part, i).start()
-
-        @pl.when(keeps == 1)
+        @pl.when(jnp.logical_not(keeps))
+        def _():
+            first_copy(part).start()
+
+        @pl.when(keeps)
         def _():
             local_copy(part).start()
 
-    def pass_copy(part, i, start):
+    def pass_copy(part, i, j, holder):
         return pltpu.make_async_remote_copy(
-            src_ref=gathered[part].at[pl.ds(start, 2)], dst_ref=gathered[part].at[pl.ds(start, 2)],
-            send_sem=pass_send.at[part, i], recv_sem=pass_recv.at[part, i],
-            device_id=(2 * lax.rem(my_y + i, 4) + my_z, col), device_id_type=MESH,
+            src_ref=gathered[part].at[holder], dst_ref=gathered[part].at[holder],
+            send_sem=pass_send.at[part, 2 * i + j], recv_sem=pass_recv.at[part, 2 * i + j],
+            device_id=place(peer(i, j)), device_id_type=MESH,
         )
 
     def pass_on(part):
-        for k in range(2):
-            @pl.when(sources[k] != me)
-            def _():
-                pltpu.make_async_remote_copy(
-                    src_ref=block[part], dst_ref=gathered[part].at[held + k],
-                    send_sem=first_send.at[part, 0], recv_sem=first_recv.at[part, k],
-                    device_id=place(sources[k]), device_id_type=MESH,
-                ).wait_recv()
-
-        @pl.when(keeps == 1)
+        @pl.when(source != me)
+        def _():
+            pltpu.make_async_remote_copy(
+                src_ref=block[part], dst_ref=gathered[part].at[held],
+                send_sem=first_send.at[part], recv_sem=first_recv.at[part],
+                device_id=place(source), device_id_type=MESH,
+            ).wait_recv()
+
+        @pl.when(source == me)
         def _():
             local_copy(part).wait()
 
-        for i in range(1, 4):
-            pass_copy(part, i, held).start()
+        for i, j in peers:
+            pass_copy(part, i, j, held).start()
 
     def finish(part, pooled):
         tokens = TOKENS[part]
         normed = token_normed(pooled, gain[...].reshape(1, TW).astype(jnp.float32))
         right = dot_nt(normed, w_right[...])
-        quarter = tokens // 4
-        lane = lax.broadcasted_iota(jnp.int32, (quarter, CZ), 1)
-        packed = right[:quarter, CZ:]
-        for m in range(1, 4):
-            packed = jnp.where(lane // CO == m, right[quarter * m : quarter * m + quarter, CZ:], packed)
-        empty = jnp.zeros((BLOCK[part] - tokens - quarter, CZ), jnp.float32)
+        lane = lax.broadcasted_iota(jnp.int32, (16, CZ), 1)
+        packed = []
+        for m in range(tokens // 16):
+            rows = right[16 * m : 16 * m + 16, CZ:]
+            if m % 4 == 0:
+                packed.append(rows)
+            else:
+                packed[-1] = jnp.where(lane // CO == m % 4, rows, packed[-1])
+        packed = jnp.concatenate(packed, axis=0)
         block[part][:tokens, :] = right[:, :CZ].astype(jnp.bfloat16)
-        block[part][tokens:, :] = jnp.concatenate([packed, empty], axis=0).astype(jnp.bfloat16)
+        block[part][tokens:, :] = packed.astype(jnp.bfloat16)
         return normed
 
-    hidden_rows(GROUP, ATOMS_DEV - GROUP, turned_atoms, att, w_out_t, w_token_t, hid)
-    pooled = pooled_rows(EDGE, TOKENS[0], GROUP, ATOMS_DEV - GROUP, me, token, hid)
-    inner = finish(0, pooled)
-
-    @pl.when(late_targets == 0)
-    def _():
-        first_sends(0)
+    def early_sends(part):
+        @pl.when(jnp.logical_not(late_target))
+        def _():
+            first_sends(part)
+
+    normed = []
+    for part, (last, lo, hi, first, number, start, stop) in enumerate(INNER):
+        for unit in inner_units:
+            if unit == last:
+                break
+        hidden_rows(lo, hi, turned_atoms, att, w_out_t, w_token_t, hid)
+        normed.append(finish(part, pooled_rows(first, number, start, stop, me, token, hid)))
+        early_sends(part)
 
     @pl.when(jnp.logical_not(is_last))
     def _():
@@ -437,18 +454,17 @@
     keep_product(ATOMS_DEV, NEXT, dot_nt(left_side, x))
     rest = jnp.concatenate([ext[ATOMS_DEV:, :], pad], axis=0)
     values[0, :AW, ATOMS_DEV:] = dot_nt(value_t, rest).astype(jnp.bfloat16)
-    attend([0, UNITS, UNITS - 1], me, off, note_in, keys, queries, values, att, mixed)
+    for _ in attend([0, UNITS, UNITS - 1], me, off, note_in, keys, queries, values, att, mixed):
+        pass
 
     hidden_rows(0, GROUP, turned_atoms, att, w_out_t, w_token_t, hid)
     hidden_rows(ATOMS_DEV - GROUP, WIDTH, turned_atoms, att, w_out_t, w_token_t, hid)
     low = pooled_rows(0, EDGE, 0, 256, me, token, hid)
     flags = note_in[:1, :].astype(jnp.float32)
     high = pooled_rows(TOK_DEV - EDGE, EDGE, ATOMS_DEV - 256, ATOMS_DEV, me, token, hid, flags)
-    outer = finish(1, jnp.concatenate([low, high], axis=0))
-
-    @pl.when(late_targets == 0)
-    def _():
-        first_sends(1)
+    outer = finish(PARTS - 1, jnp.concatenate([low, high], axis=0))
+
+    early_sends(PARTS - 1)
 
     def left_copy(source, to, index):
         return pltpu.make_async_remote_copy(
@@ -461,8 +477,8 @@
 
     @pl.when(is_first)
     def _():
-        normed = jnp.concatenate([outer[:EDGE], inner[: HALF - EDGE]], axis=0)
-        left = dot_nt(normed, w_pair[: 2 * CZ, :])
+        first_rows = jnp.concatenate([outer[:EDGE], normed[0][: HALF - EDGE]], axis=0)
+        left = dot_nt(first_rows, w_pair[: 2 * CZ, :])
         for r in range(ROWS):
             rows = left[8 * r : 8 * r + 8]
             left_all[r] = jnp.concatenate([rows[:, :CZ], rows[:, CZ:]], axis=0).astype(jnp.bfloat16)
@@ -476,11 +492,11 @@
 
     each_head(lambda to, index: left_to(to, index).start())
 
-    @pl.when(late_targets != 0)
-    def _():
-        pl.semaphore_wait(far_ready, late_targets)
-        first_sends(0)
-        first_sends(1)
+    @pl.when(late_target)
+    def _():
+        pl.semaphore_wait(far_ready, 1)
+        for part in range(PARTS):
+            first_sends(part)
 
     @pl.when(is_head & jnp.logical_not(is_leader))
     def _():
@@ -491,8 +507,8 @@
         pl.semaphore_wait(left_ready, children)
 
     each_child(lambda to, index: left_to(to, index).start())
-    pass_on(0)
-    pass_on(1)
+    for part in range(PARTS):
+        pass_on(part)
 
     @pl.when(child)
     def _():
@@ -501,16 +517,10 @@
     mix_left(left_in, w_outer, base)
     left = left_in[:8, :].astype(jnp.float32)
 
-    def arrived(part):
-        for i in range(1, 4):
-            theirs = held_by(my_y + 4 - i)
-            pass_copy(part, i, theirs).wait_recv()
-            pair_block(gathered[part], part, theirs, base, left, result)
-
-    pair_block(gathered[0], 0, held, base, left, result)
-    arrived(0)
-    pair_block(gathered[1], 1, held, base, left, result)
-    arrived(1)
+    for part in range(PARTS):
+        for i, j in peers:
+            pass_copy(part, i, j, held_by(my_y + 4 - i, lax.rem(my_z + j, 2))).wait_recv()
+        pair_part(gathered[part], part, base, left, result)
 
     for each in (each_leader, each_head, each_child):
         each(lambda to, index: left_to(to, index).wait_send())
@@ -524,13 +534,13 @@
         for copy in to_before:
             copy.wait_send()
 
-    for part in range(2):
-        for i in range(1, 4):
-            pass_copy(part, i, held).wait_send()
-        for i in range(2):
-            @pl.when(targets[i] != me)
-            def _():
-                first_copy(part, i).wait_send()
+    for part in range(PARTS):
+        for i, j in peers:
+            pass_copy(part, i, j, held).wait_send()
+
+        @pl.when(jnp.logical_not(keeps))
+        def _():
+            first_copy(part).wait_send()
 
 
 def mix_left(left_in, w_outer, base):
@@ -547,25 +557,32 @@
             base[CZ + CO * k : CZ + CO * k + CO, CZ * i : CZ * i + CZ] = mixing[CO * i : CO * i + CO]
 
 
-def pair_block(gathered, part, start, base, left, result):
-    tokens, quarter = TOKENS[part], TOKENS[part] // 4
-    lane = lax.broadcasted_iota(jnp.int32, (quarter, CZ), 1)
+def packed_rows(tokens):
+    return 16 * -(-tokens // 64)
+
+
+def pair_part(gathered, part, base, left, result):
+    tokens = TOKENS[part]
+    lane = lax.broadcasted_iota(jnp.int32, (16, CZ), 1)
     pieces = []
-    for k in range(2):
-        packed = gathered[start + k, tokens:, :].astype(jnp.float32)[:quarter]
-        outer = [jnp.where(lane // CO == m, packed, 0.0) for m in range(4)]
+    for k in range(ROWS):
+        packed = gathered[k, tokens:, :].astype(jnp.float32)
+        outer = [
+            jnp.where(lane // CO == m % 4, packed[16 * (m // 4) : 16 * (m // 4) + 16], 0.0)
+            for m in range(tokens // 16)
+        ]
         outer = jnp.concatenate(outer, axis=0).astype(jnp.bfloat16)
-        pieces.append(jnp.concatenate([gathered[start + k, :tokens, :], outer], axis=1))
+        pieces.append(jnp.concatenate([gathered[k, :tokens, :], outer], axis=1))
     rows = jnp.concatenate(pieces, axis=0)
-    spans = [(0, EDGE, tokens)] if part == 0 else [(0, 0, EDGE), (EDGE, TOK_DEV - EDGE, EDGE)]
     for i in range(0, 8, 2):
         grid = dot(rows, base[:, CZ * i : CZ * i + 2 * CZ])
         for j in range(2):
             total = (grid[:, CZ * j : CZ * j + CZ] + left[i + j : i + j + 1]).astype(jnp.bfloat16)
-            for k in range(2):
-                for first, to, size in spans:
-                    target = pl.multiple_of(TOK_DEV * (start + k) + to, EDGE)
-                    result[i + j, pl.ds(target, size), :] = total[tokens * k + first : tokens * k + first + size]
+            for k in range(ROWS):
+                for first, to, size in SPANS[part]:
+                    to += TOK_DEV * k
+                    first += tokens * k
+                    result[i + j, to : to + size, :] = total[first : first + size]
 
 
 def body(
@@ -590,8 +607,7 @@
             pltpu.VMEM((TW,), bf16),
             pltpu.VMEM((2 * CZ + 2 * CO, TW), bf16),
             pltpu.VMEM((CO * CO, CZ), bf16),
-            pltpu.VMEM((ROWS, BLOCK[0], CZ), bf16),
-            pltpu.VMEM((ROWS, BLOCK[1], CZ), bf16),
+            *[pltpu.VMEM((ROWS, tokens + packed_rows(tokens), CZ), bf16) for tokens in TOKENS],
             pltpu.VMEM((2 * CZ, 8 * CZ), bf16),
             pltpu.VMEM((EXT, AW), bf16),
             pltpu.VMEM((EXT, AW), bf16),
@@ -605,12 +621,11 @@
             pltpu.VMEM((2 * CZ, TW), bf16),
             pltpu.VMEM((16, NEXT), bf16),
             pltpu.VMEM((16, NEXT), bf16),
-            pltpu.VMEM((BLOCK[0], CZ), bf16),
-            pltpu.VMEM((BLOCK[1], CZ), bf16),
+            *[pltpu.VMEM((tokens + packed_rows(tokens), CZ), bf16) for tokens in TOKENS],
             pltpu.VMEM((ROWS, 16, CZ), bf16),
             pltpu.VMEM((16, CZ), bf16),
             dma, dma((10,)), dma((3,)), dma((3,)),
-            dma((2, 2)), dma((2, 2)), dma((2,)), dma((2, 4)), dma((2, 4)), dma((COLS,)), dma,
+            dma((PARTS,)), dma((PARTS,)), dma((PARTS,)), dma((PARTS, ROWS)), dma((PARTS, ROWS)), dma((COLS,)), dma,
             pltpu.SemaphoreType.REGULAR, pltpu.SemaphoreType.REGULAR,
         ],
         compiler_params=pltpu.CompilerParams(

time: 30 us -> 27.2 us (0.907)
  the two profiles are of different devices: /device:TPU:65 before, /device:TPU:64 now
where the time goes in v6:
time: 27.2 us; the launch traced here: 27.1 us
  Pallas kernels  25.7 us (94%)
  local copies, waits for them, and re-layouts  1.32 us (5%)
    pallas_call x1, Pallas kernels, body(): pl.pallas_call(embed_kernel, out_shape=pltpu.VMEM((8, ROWS * TOK_DEV, CZ)...  25.7 us
    unnamed x1, local copies, waits for them, and re-layouts  1.32 us

profile of v6, /device:TPU:64, one launch (start us, length us, event | category | flops | bytes accessed | tf_op | source)
XLA Modules:
  0.0 27.1 jit_solution(1175641711427392726)
XLA Ops:
  0.0 25.7 %embed.1 = bf16[8,1024,128]{2,1,0:T(8,128)(2,1)S(1)} custom-call(bf16[1536,128]{1,0:T(8,128)(2,1)} %atoms.1, s32[48]{0:T(128)} %off_hbm.1, s32[1536]{0:T(1024)} %token_hbm.1, bf16[128,128]{1,0:T(8,128)(2,1)} %wq_hbm.1, bf16[128,128]{1,0:T(8,128)(2,1)} %wk_hbm.1, bf16[128,128]{1,0:T(8,128)(2,1)} %wv_hbm.1, bf16[128,128]{1,0:T(8,128)(2,1)} %w_out_hbm.1, ...), custom_call_target="tpu_custom_call" | custom-call | tf_op jit(solution)/shard_map/embed/pallas_call | solution.py:594
  25.8 1.3 %copy.13 = bf16[8,1024,128]{2,1,0:T(8,128)(2,1)} copy(bf16[8,1024,128]{2,1,0:T(8,128)(2,1)S(1)} %embed.1) | data formatting | bytes 4194304

commit v7 on v6

--- a/solution.py
+++ b/solution.py
@@ -159,7 +159,7 @@
     ext, keys, queries, values, att, hid, turned_atoms, w_out_t, w_token_t, w_right,
     note_out, note_in, block0, block1, left_all, left_in,
     own_sem, load_sem, halo_send, halo_recv,
-    first_send, first_recv, local_sem, pass_send, pass_recv, left_send, left_recv, far_ready, left_ready,
+    first_send, first_recv, local_sem, pass_send, pass_recv, left_send, left_recv, far_ready, left_ready, pass_ready,
 ):
     gathered, block = (gathered0, gathered1), (block0, block1)
     row = lax.axis_index("row")
@@ -172,19 +172,19 @@
     my_x, my_zh = lax.div(col, 8), lax.rem(lax.div(col, 2), 4)
     depth = 2 * my_zh + my_z
     group_col = lax.div(me, ROWS)
-    relay_y = lax.rem(my_y + 6 + my_zh - 2 * my_z - lax.div(my_x, 2), 4)
+    relay_y = lax.rem(my_y + 6 + my_zh - 2 * my_z - lax.div(my_x, 2) + 2 * lax.rem(my_x, 2), 4)
     my_core = lax.rem(col, 2)
     target = (2 * relay_y + my_core) * COLS + group_col
     target_depth = 4 * my_z + 2 * lax.div(my_x, 2) + my_core
 
     def held_by(y, z):
-        return 2 * lax.rem(y + 6 + my_zh - my_x, 4) + z
+        return 2 * lax.rem(y + 6 + my_zh - my_x + 2 * my_core, 4) + z
 
     held = held_by(my_y, my_z)
     source = ROWS * col + held
     source_depth = 2 * lax.div(held, 2) + lax.div(my_zh, 2)
     keeps = target == me
-    peers = [(i, j) for i in range(4) for j in range(2) if i + j > 0]
+    peers = [(2, 1), (2, 0), (1, 1), (3, 1), (1, 0), (3, 0), (0, 1)]
     col_in = lax.rem(col, 8)
     is_head, is_leader, is_first, is_last = col_in == 1, col == 1, me == 0, me == DEVICES - 1
     parent = jnp.where(is_leader, 0, jnp.where(is_head, row * COLS + 1, me - col_in + 1))
@@ -197,8 +197,12 @@
             barrier if semaphore is None else semaphore, inc=1, device_id=place(device), device_id_type=MESH
         )
 
-    own = pltpu.make_async_copy(atoms, ext.at[pl.ds(RIM, ATOMS_DEV)], own_sem)
-    own.start()
+    own = [
+        pltpu.make_async_copy(atoms.at[pl.ds(lo, 512)], ext.at[pl.ds(RIM + lo, 512)], own_sem.at[lo // 512])
+        for lo in range(0, ATOMS_DEV, 512)
+    ]
+    for copy in own:
+        copy.start()
     pieces = [
         (wq_hbm, wq), (wk_hbm, wk), (wv_hbm, wv), (off_hbm, off), (w_out_hbm, w_out),
         (token_hbm, token), (w_token_hbm, w_token), (gain_hbm, gain), (w_pair_hbm, w_pair),
@@ -240,8 +244,10 @@
         return (2 * lax.rem(my_y + i, 4) + lax.rem(my_z + j, 2)) * COLS + col
 
     for i, j in peers:
-        signal(peer(i, j))
-    arrivals += len(peers)
+        @pl.when(peer(i, j) > me)
+        def _():
+            signal(peer(i, j))
+    arrivals += row
     child = jnp.logical_not(is_head | is_first)
     arrivals += count(child)
     children = 7 - count((row == 0) & is_leader)
@@ -277,10 +283,6 @@
     hid[TW:, :] = jnp.ones((WIDE - TW, WIDTH), jnp.bfloat16)
     for j in range(2):
         values[j, AW:, :] = jnp.ones((16, WIDTH + GROUP), jnp.bfloat16)
-    own.wait()
-    for lo in range(0, ATOMS_DEV, 512):
-        x = ext[RIM + lo : RIM + lo + 512, :]
-        keys[RIM + lo : RIM + lo + 512, :] = dot(x, wk[...]).astype(jnp.bfloat16)
     def keep_product(lo, size, product):
         for h in range(HEADS):
             rows = slice(32 * h, 32 * h + 32)
@@ -292,15 +294,12 @@
         values[1, :AW, lo : lo + size] = product[AW : 2 * AW].astype(jnp.bfloat16)
         turned_atoms[:, lo : lo + size] = product[2 * AW :].astype(jnp.bfloat16)
 
-    for lo in range(0, ATOMS_DEV, 256):
-        keep_product(lo, 256, dot_nt(left_side, ext[RIM + lo : RIM + lo + 256, :]))
-    for lo in range(128, ATOMS_DEV, 256):
-        hi = min(lo + 256, ATOMS_DEV)
-        values[0, :AW, lo:hi] = dot_nt(value_t, ext[lo:hi, :]).astype(jnp.bfloat16)
-    pad = jnp.zeros((RIM, AW), jnp.bfloat16)
-    rest = jnp.concatenate([ext[ATOMS_DEV : ATOMS_DEV + RIM, :], pad], axis=0)
-    values[0, :AW, ATOMS_DEV : ATOMS_DEV + GROUP] = dot_nt(value_t, rest).astype(jnp.bfloat16)
-
+    for lo in range(0, ATOMS_DEV, 512):
+        own[lo // 512].wait()
+        x = ext[RIM + lo : RIM + lo + 512, :]
+        keys[RIM + lo : RIM + lo + 512, :] = dot(x, wk[...]).astype(jnp.bfloat16)
+        for part in range(0, 512, 256):
+            keep_product(lo + part, 256, dot_nt(left_side, x[part : part + 256]))
     for load in loads[3:]:
         load.wait()
     flags = token[...].reshape(1, ATOMS_DEV)[:, :NEXT] == me * TOK_DEV - 1
@@ -319,14 +318,6 @@
         note_in[...] = jnp.zeros((16, NEXT), jnp.bfloat16)
 
     pl.semaphore_wait(barrier, arrivals)
-
-    @pl.when((source != me) & (source_depth < depth))
-    def _():
-        signal(source, far_ready)
-
-    @pl.when(child)
-    def _():
-        signal(parent, left_ready)
 
     to_after = pltpu.make_async_remote_copy(
         src_ref=atoms.at[pl.ds(ATOMS_DEV - RIM, RIM)], dst_ref=ext.at[pl.ds(0, RIM)],
@@ -354,6 +345,26 @@
         for copy in to_before:
             copy.start()
 
+    @pl.when((source != me) & (source_depth < depth))
+    def _():
+        signal(source, far_ready)
+
+    @pl.when(child)
+    def _():
+        signal(parent, left_ready)
+
+    for i, j in peers:
+        @pl.when(peer(i, j) < me)
+        def _():
+            signal(peer(i, j), pass_ready)
+
+    for lo in range(128, ATOMS_DEV, 256):
+        hi = min(lo + 256, ATOMS_DEV)
+        values[0, :AW, lo:hi] = dot_nt(value_t, ext[lo:hi, :]).astype(jnp.bfloat16)
+    pad = jnp.zeros((RIM, AW), jnp.bfloat16)
+    rest = jnp.concatenate([ext[ATOMS_DEV : ATOMS_DEV + RIM, :], pad], axis=0)
+    values[0, :AW, ATOMS_DEV : ATOMS_DEV + GROUP] = dot_nt(value_t, rest).astype(jnp.bfloat16)
+
     for i in range(8):
         base[:CZ, CZ * i : CZ * i + CZ] = eye
     w_out_t[...] = turned(w_out)
@@ -507,6 +518,10 @@
         pl.semaphore_wait(left_ready, children)
 
     each_child(lambda to, index: left_to(to, index).start())
+    @pl.when(row < ROWS - 1)
+    def _():
+        pl.semaphore_wait(pass_ready, ROWS - 1 - row)
+
     for part in range(PARTS):
         pass_on(part)
 
@@ -624,9 +639,9 @@
             *[pltpu.VMEM((tokens + packed_rows(tokens), CZ), bf16) for tokens in TOKENS],
             pltpu.VMEM((ROWS, 16, CZ), bf16),
             pltpu.VMEM((16, CZ), bf16),
-            dma, dma((10,)), dma((3,)), dma((3,)),
+            dma((3,)), dma((10,)), dma((3,)), dma((3,)),
             dma((PARTS,)), dma((PARTS,)), dma((PARTS,)), dma((PARTS, ROWS)), dma((PARTS, ROWS)), dma((COLS,)), dma,
-            pltpu.SemaphoreType.REGULAR, pltpu.SemaphoreType.REGULAR,
+            *[pltpu.SemaphoreType.REGULAR] * 3,
         ],
         compiler_params=pltpu.CompilerParams(
             collective_id=0, has_side_effects=True, vmem_limit_bytes=60 * 1024 * 1024

time: 27.2 us -> 25.7 us (0.945)
  the two profiles are of different devices: /device:TPU:64 before, /device:TPU:65 now
where the time goes in v7:
time: 25.7 us; the launch traced here: 25.3 us
  Pallas kernels  24 us (93%)
  local copies, waits for them, and re-layouts  1.32 us (5%)
    pallas_call x1, Pallas kernels, body(): pl.pallas_call(embed_kernel, out_shape=pltpu.VMEM((8, ROWS * TOK_DEV, CZ)...  24 us
    unnamed x1, local copies, waits for them, and re-layouts  1.32 us

profile of v7, /device:TPU:65, one launch (start us, length us, event | category | flops | bytes accessed | tf_op | source)
XLA Modules:
  0.0 25.3 jit_solution(8311500628068345537)
XLA Ops:
  0.0 24.0 %embed.1 = bf16[8,1024,128]{2,1,0:T(8,128)(2,1)S(1)} custom-call(bf16[1536,128]{1,0:T(8,128)(2,1)} %atoms.1, s32[48]{0:T(128)} %off_hbm.1, s32[1536]{0:T(1024)} %token_hbm.1, bf16[128,128]{1,0:T(8,128)(2,1)} %wq_hbm.1, bf16[128,128]{1,0:T(8,128)(2,1)} %wk_hbm.1, bf16[128,128]{1,0:T(8,128)(2,1)} %wv_hbm.1, bf16[128,128]{1,0:T(8,128)(2,1)} %w_out_hbm.1, ...), custom_call_target="tpu_custom_call" | custom-call | tf_op jit(solution)/shard_map/embed/pallas_call | solution.py:609
  24.0 1.3 %copy.13 = bf16[8,1024,128]{2,1,0:T(8,128)(2,1)} copy(bf16[8,1024,128]{2,1,0:T(8,128)(2,1)S(1)} %embed.1) | data formatting | bytes 4194304

commit v8 on v7

--- a/solution.py
+++ b/solution.py
@@ -398,8 +398,15 @@
     def pass_copy(part, i, j, holder):
         return pltpu.make_async_remote_copy(
             src_ref=gathered[part].at[holder], dst_ref=gathered[part].at[holder],
-            send_sem=pass_send.at[part, 2 * i + j], recv_sem=pass_recv.at[part, 2 * i + j],
+            send_sem=pass_send.at[part], recv_sem=pass_recv.at[part],
             device_id=place(peer(i, j)), device_id_type=MESH,
+        )
+
+    def pass_all(part):
+        blocks = gathered[part].at[pl.ds(0, ROWS - 1)]
+        return pltpu.make_async_remote_copy(
+            src_ref=blocks, dst_ref=blocks, send_sem=pass_send.at[part], recv_sem=pass_recv.at[part],
+            device_id=place(peer(0, 1)), device_id_type=MESH,
         )
 
     def pass_on(part):
@@ -484,7 +491,14 @@
         )
 
     def left_to(child, index):
-        return left_copy(left_all.at[index] if index < ROWS else left_in, child, index)
+        return left_copy(left_all.at[index] if index < ROWS else left_in, child, index // 8)
+
+    def left_sent(count, index):
+        rows = left_all.at[pl.ds(0, count)]
+        return pltpu.make_async_remote_copy(
+            src_ref=rows, dst_ref=rows, send_sem=left_send.at[index], recv_sem=left_recv,
+            device_id=place(parent), device_id_type=MESH,
+        ).wait_send()
 
     @pl.when(is_first)
     def _():
@@ -533,12 +547,24 @@
     left = left_in[:8, :].astype(jnp.float32)
 
     for part in range(PARTS):
-        for i, j in peers:
-            pass_copy(part, i, j, held_by(my_y + 4 - i, lax.rem(my_z + j, 2))).wait_recv()
+        pass_all(part).wait_recv()
         pair_part(gathered[part], part, base, left, result)
 
-    for each in (each_leader, each_head, each_child):
-        each(lambda to, index: left_to(to, index).wait_send())
+    @pl.when(is_first)
+    def _():
+        left_sent(8, 0)
+
+    @pl.when(is_leader)
+    def _():
+        left_sent(3, 1)
+
+    @pl.when(is_head & (me != 1))
+    def _():
+        left_sent(7, 2)
+
+    @pl.when(me == 1)
+    def _():
+        left_sent(6, 2)
 
     @pl.when(jnp.logical_not(is_last))
     def _():
@@ -550,8 +576,7 @@
             copy.wait_send()
 
     for part in range(PARTS):
-        for i, j in peers:
-            pass_copy(part, i, j, held).wait_send()
+        pass_all(part).wait_send()
 
         @pl.when(jnp.logical_not(keeps))
         def _():
@@ -640,7 +665,7 @@
             pltpu.VMEM((ROWS, 16, CZ), bf16),
             pltpu.VMEM((16, CZ), bf16),
             dma((3,)), dma((10,)), dma((3,)), dma((3,)),
-            dma((PARTS,)), dma((PARTS,)), dma((PARTS,)), dma((PARTS, ROWS)), dma((PARTS, ROWS)), dma((COLS,)), dma,
+            dma((PARTS,)), dma((PARTS,)), dma((PARTS,)), dma((PARTS,)), dma((PARTS,)), dma((3,)), dma,
             *[pltpu.SemaphoreType.REGULAR] * 3,
         ],
         compiler_params=pltpu.CompilerParams(

time: 25.7 us -> 25.2 us (0.981)
  Pallas kernels: 24 us -> 23.4 us
    pallas_call x1, Pallas kernels: 24 us -> 23.4 us  [body(): pl.pallas_call(embed_kernel, out_shape=pltpu.VMEM((8, ROWS * TOK_DEV, CZ)...]
where the time goes in v8:
time: 25.2 us; the launch traced here: 24.8 us
  Pallas kernels  23.4 us (93%)
  local copies, waits for them, and re-layouts  1.32 us (5%)
    pallas_call x1, Pallas kernels, body(): pl.pallas_call(embed_kernel, out_shape=pltpu.VMEM((8, ROWS * TOK_DEV, CZ)...  23.4 us
    unnamed x1, local copies, waits for them, and re-layouts  1.32 us

profile of v8, /device:TPU:65, one launch (start us, length us, event | category | flops | bytes accessed | tf_op | source)
XLA Modules:
  0.0 24.8 jit_solution(8291507746046855530)
XLA Ops:
  0.0 23.4 %embed.1 = bf16[8,1024,128]{2,1,0:T(8,128)(2,1)S(1)} custom-call(bf16[1536,128]{1,0:T(8,128)(2,1)} %atoms.1, s32[48]{0:T(128)} %off_hbm.1, s32[1536]{0:T(1024)} %token_hbm.1, bf16[128,128]{1,0:T(8,128)(2,1)} %wq_hbm.1, bf16[128,128]{1,0:T(8,128)(2,1)} %wk_hbm.1, bf16[128,128]{1,0:T(8,128)(2,1)} %wv_hbm.1, bf16[128,128]{1,0:T(8,128)(2,1)} %w_out_hbm.1, ...), custom_call_target="tpu_custom_call" | custom-call | tf_op jit(solution)/shard_map/embed/pallas_call | solution.py:634
  23.4 1.3 %copy.13 = bf16[8,1024,128]{2,1,0:T(8,128)(2,1)} copy(bf16[8,1024,128]{2,1,0:T(8,128)(2,1)S(1)} %embed.1) | data formatting | bytes 4194304

commit v9 on v8

--- a/solution.py
+++ b/solution.py
@@ -204,8 +204,8 @@
     for copy in own:
         copy.start()
     pieces = [
-        (wq_hbm, wq), (wk_hbm, wk), (wv_hbm, wv), (off_hbm, off), (w_out_hbm, w_out),
-        (token_hbm, token), (w_token_hbm, w_token), (gain_hbm, gain), (w_pair_hbm, w_pair),
+        (wq_hbm, wq), (wk_hbm, wk), (wv_hbm, wv), (off_hbm, off), (token_hbm, token),
+        (w_out_hbm, w_out), (w_token_hbm, w_token), (gain_hbm, gain), (w_pair_hbm, w_pair),
         (w_outer_hbm, w_outer),
     ]
     loads = [pltpu.make_async_copy(a, b, load_sem.at[i]) for i, (a, b) in enumerate(pieces)]
@@ -300,7 +300,7 @@
         keys[RIM + lo : RIM + lo + 512, :] = dot(x, wk[...]).astype(jnp.bfloat16)
         for part in range(0, 512, 256):
             keep_product(lo + part, 256, dot_nt(left_side, x[part : part + 256]))
-    for load in loads[3:]:
+    for load in loads[3:5]:
         load.wait()
     flags = token[...].reshape(1, ATOMS_DEV)[:, :NEXT] == me * TOK_DEV - 1
     upper = lax.broadcasted_iota(jnp.int32, (16, NEXT), 0) < 8
@@ -365,6 +365,8 @@
     rest = jnp.concatenate([ext[ATOMS_DEV : ATOMS_DEV + RIM, :], pad], axis=0)
     values[0, :AW, ATOMS_DEV : ATOMS_DEV + GROUP] = dot_nt(value_t, rest).astype(jnp.bfloat16)
 
+    for load in loads[5:]:
+        load.wait()
     for i in range(8):
         base[:CZ, CZ * i : CZ * i + CZ] = eye
     w_out_t[...] = turned(w_out)

time: 25.2 us -> 25.2 us (level)
  no operation moved by 1% of the time
where the time goes in v9:
time: 25.2 us; the launch traced here: 24.8 us
  Pallas kernels  23.5 us (93%)
  local copies, waits for them, and re-layouts  1.32 us (5%)
    pallas_call x1, Pallas kernels, body(): pl.pallas_call(embed_kernel, out_shape=pltpu.VMEM((8, ROWS * TOK_DEV, CZ)...  23.5 us
    unnamed x1, local copies, waits for them, and re-layouts  1.32 us

profile of v9, /device:TPU:65, one launch (start us, length us, event | category | flops | bytes accessed | tf_op | source)
XLA Modules:
  0.0 24.8 jit_solution(3111956768261065137)
XLA Ops:
  0.0 23.5 %embed.1 = bf16[8,1024,128]{2,1,0:T(8,128)(2,1)S(1)} custom-call(bf16[1536,128]{1,0:T(8,128)(2,1)} %atoms.1, s32[48]{0:T(128)} %off_hbm.1, s32[1536]{0:T(1024)} %token_hbm.1, bf16[128,128]{1,0:T(8,128)(2,1)} %wq_hbm.1, bf16[128,128]{1,0:T(8,128)(2,1)} %wk_hbm.1, bf16[128,128]{1,0:T(8,128)(2,1)} %wv_hbm.1, bf16[128,128]{1,0:T(8,128)(2,1)} %w_out_hbm.1, ...), custom_call_target="tpu_custom_call" | custom-call | tf_op jit(solution)/shard_map/embed/pallas_call | solution.py:636
  23.5 1.3 %copy.13 = bf16[8,1024,128]{2,1,0:T(8,128)(2,1)} copy(bf16[8,1024,128]{2,1,0:T(8,128)(2,1)S(1)} %embed.1) | data formatting | bytes 4194304

commit v10 on v9

--- a/solution.py
+++ b/solution.py
@@ -197,6 +197,15 @@
             barrier if semaphore is None else semaphore, inc=1, device_id=place(device), device_id_type=MESH
         )
 
+    barrier = pltpu.get_barrier_semaphore()
+    @pl.when(jnp.logical_not(is_first))
+    def _():
+        signal(before)
+
+    @pl.when(jnp.logical_not(is_last))
+    def _():
+        signal(after)
+
     own = [
         pltpu.make_async_copy(atoms.at[pl.ds(lo, 512)], ext.at[pl.ds(RIM + lo, 512)], own_sem.at[lo // 512])
         for lo in range(0, ATOMS_DEV, 512)
@@ -212,15 +221,6 @@
     for load in loads:
         load.start()
 
-    barrier = pltpu.get_barrier_semaphore()
-
-    @pl.when(jnp.logical_not(is_first))
-    def _():
-        signal(before)
-
-    @pl.when(jnp.logical_not(is_last))
-    def _():
-        signal(after)
 
     @pl.when(is_head)
     def _():
@@ -294,7 +294,7 @@
         values[1, :AW, lo : lo + size] = product[AW : 2 * AW].astype(jnp.bfloat16)
         turned_atoms[:, lo : lo + size] = product[2 * AW :].astype(jnp.bfloat16)
 
-    for lo in range(0, ATOMS_DEV, 512):
+    for lo in range(0, 512, 512):
         own[lo // 512].wait()
         x = ext[RIM + lo : RIM + lo + 512, :]
         keys[RIM + lo : RIM + lo + 512, :] = dot(x, wk[...]).astype(jnp.bfloat16)
@@ -358,6 +358,12 @@
         def _():
             signal(peer(i, j), pass_ready)
 
+    for lo in range(512, ATOMS_DEV, 512):
+        own[lo // 512].wait()
+        x = ext[RIM + lo : RIM + lo + 512, :]
+        keys[RIM + lo : RIM + lo + 512, :] = dot(x, wk[...]).astype(jnp.bfloat16)
+        for part in range(0, 512, 256):
+            keep_product(lo + part, 256, dot_nt(left_side, x[part : part + 256]))
     for lo in range(128, ATOMS_DEV, 256):
         hi = min(lo + 256, ATOMS_DEV)
         values[0, :AW, lo:hi] = dot_nt(value_t, ext[lo:hi, :]).astype(jnp.bfloat16)

time: 25.2 us -> 24.9 us (0.988); the launches traced: 24.8 us -> 24.8 us
  no operation moved by 1% of the time
where the time goes in v10:
time: 24.9 us; the launch traced here: 24.8 us
  Pallas kernels  23.5 us (94%)
  local copies, waits for them, and re-layouts  1.32 us (5%)
    pallas_call x1, Pallas kernels, body(): pl.pallas_call(embed_kernel, out_shape=pltpu.VMEM((8, ROWS * TOK_DEV, CZ)...  23.5 us
    unnamed x1, local copies, waits for them, and re-layouts  1.32 us

profile of v10, /device:TPU:65, one launch (start us, length us, event | category | flops | bytes accessed | tf_op | source)
XLA Modules:
  0.0 24.8 jit_solution(3916200352653460681)
XLA Ops:
  0.0 23.5 %embed.1 = bf16[8,1024,128]{2,1,0:T(8,128)(2,1)S(1)} custom-call(bf16[1536,128]{1,0:T(8,128)(2,1)} %atoms.1, s32[48]{0:T(128)} %off_hbm.1, s32[1536]{0:T(1024)} %token_hbm.1, bf16[128,128]{1,0:T(8,128)(2,1)} %wq_hbm.1, bf16[128,128]{1,0:T(8,128)(2,1)} %wk_hbm.1, bf16[128,128]{1,0:T(8,128)(2,1)} %wv_hbm.1, bf16[128,128]{1,0:T(8,128)(2,1)} %w_out_hbm.1, ...), custom_call_target="tpu_custom_call" | custom-call | tf_op jit(solution)/shard_map/embed/pallas_call | solution.py:642
  23.5 1.3 %copy.13 = bf16[8,1024,128]{2,1,0:T(8,128)(2,1)} copy(bf16[8,1024,128]{2,1,0:T(8,128)(2,1)S(1)} %embed.1) | data formatting | bytes 4194304
